TPU v7x, 256 devices: a whole 4x4x8 slice. The times are simulated.
256 devices in a mesh: expert: 32 (over y, z), dp: 8 (over x, core).
Axes of the slice: x: 4, y: 4, z: 8, core: 2. Of those that a mesh axis runs over, the one named last changes fastest.
Arguments:
- tokens: bfloat16 [32768, 1024], P(('expert', 'dp')), may hold values from -6 to 6
- out_grad: bfloat16 [32768, 1024], P(('expert', 'dp')), may hold values from -6 to 6
- expert_ids: int32 [32768, 8], P(('expert', 'dp')), may hold values from 0 to 127, all different within a row; in each aligned block of 128 rows (0 to 127, 128 to 255, ...) at most 10 rows name the same one
- gate_weights: bfloat16 [32768, 8], P(('expert', 'dp')), may hold values from 0.019897461 to 0.3984375
- keep_flags: int32 [32768], P(('expert', 'dp')), may hold values 0 or 1
- gate_proj: bfloat16 [256, 512, 640], P(('expert', 'dp')), may hold values from -0.1875 to 0.1875
- up_proj: bfloat16 [256, 512, 640], P(('expert', 'dp')), may hold values from -0.1875 to 0.1875
- down_proj: bfloat16 [256, 640, 512], P(('expert', 'dp')), may hold values from -0.25 to 0.25
Outputs:
- grad_tokens: bfloat16 [32768, 1024], P(('expert', 'dp'))
- grad_gates: bfloat16 [32768, 8], P(('expert', 'dp'))
- grad_gate_proj: bfloat16 [256, 512, 640], P(('expert', 'dp'))
- grad_up_proj: bfloat16 [256, 512, 640], P(('expert', 'dp'))
- grad_down_proj: bfloat16 [256, 640, 512], P(('expert', 'dp'))
Inputs may be any that keep to these rules, and one draw needn't show every extreme that they name: `expert_ids`: each token names 8 different experts; the 128 rows of one device name no expert more than 10 times, a bound that some block reaches.
All inputs are finite; a program needn't handle non-finite values. No bound on the sum of `keep_flags` on one device may be relied on, other than what follows from the above.
Results may differ from a plain program's by a relative error of at most 0.012.
Values may be sent and summed in bfloat16 or wider, within the bound.
A program may use at most 128 MiB of HBM per device.

v0:
```python
import jax
import jax.numpy as jnp
from jax import lax
from jax.sharding import PartitionSpec as P


def swapped(value, axis, distance):
    mask = 2**distance
    pairs = [(source, source ^ mask) for source in range(lax.axis_size(axis))]
    return lax.ppermute(value, axis, pairs)


def assemble(mine, theirs, first, axis_num):
    lower = jnp.where(first, mine, theirs)
    upper = jnp.where(first, theirs, mine)
    return jnp.concatenate([lower[0], upper[0]], axis=axis_num)


def body(tokens, out_grad, expert_ids, gate_weights, keep_flags, gate_proj, up_proj, down_proj):
    expert_count = lax.axis_size("expert")
    pair_count = lax.axis_size("dp")
    tok_rows, width = tokens.shape
    top_count = expert_ids.shape[1]
    experts_all = expert_count * pair_count // 2
    capacity = top_count * tok_rows * 5 // (4 * experts_all)
    half_slots = capacity // 2
    assigned = tok_rows * top_count
    flat_ids = expert_ids.reshape(-1)
    onehot = (flat_ids[:, None] == jnp.arange(experts_all, dtype=jnp.int32)[None, :]).astype(
        jnp.bfloat16
    )
    row_place = jnp.arange(assigned, dtype=jnp.int32)
    before = (row_place[None, :] < row_place[:, None]).astype(jnp.bfloat16)
    earlier = jnp.dot(before, onehot, preferred_element_type=jnp.float32)
    slot_index = jnp.sum(earlier * onehot.astype(jnp.float32), axis=1).astype(jnp.int32)
    destination = flat_ids * capacity + slot_index
    slot_owner = jnp.full((experts_all * capacity,), -1, jnp.int32).at[destination].set(row_place)
    live_slot = slot_owner >= 0
    source = jnp.where(live_slot, slot_owner, 0)
    source_row = source // top_count
    keep_half = keep_flags.astype(jnp.bfloat16)
    scale_half = (gate_weights * keep_half[:, None]).reshape(-1)
    zero_half = jnp.zeros((), jnp.bfloat16)
    send_scale = jnp.where(live_slot, scale_half[source], zero_half)
    send_keep = jnp.where(live_slot, keep_half[source_row], zero_half)
    layout = (expert_count, pair_count, half_slots)
    packed = (
        tokens[source_row].reshape(layout + (width,)),
        out_grad[source_row].reshape(layout + (width,)),
        send_scale.reshape(layout),
        send_keep.reshape(layout),
    )
    arrived = (
        lax.all_to_all(
            lax.all_to_all(packed[0], "expert", split_axis=0, concat_axis=0, tiled=True),
            "dp",
            split_axis=1,
            concat_axis=1,
            tiled=True,
        ),
        lax.all_to_all(
            lax.all_to_all(packed[1], "expert", split_axis=0, concat_axis=0, tiled=True),
            "dp",
            split_axis=1,
            concat_axis=1,
            tiled=True,
        ),
        lax.all_to_all(
            lax.all_to_all(packed[2], "expert", split_axis=0, concat_axis=0, tiled=True),
            "dp",
            split_axis=1,
            concat_axis=1,
            tiled=True,
        ),
        lax.all_to_all(
            lax.all_to_all(packed[3], "expert", split_axis=0, concat_axis=0, tiled=True),
            "dp",
            split_axis=1,
            concat_axis=1,
            tiled=True,
        ),
    )
    rows_x = arrived[0].reshape(-1, width)
    rows_dy = arrived[1].reshape(-1, width)
    route_scale = arrived[2].reshape(-1).astype(jnp.float32)
    keep_rows = arrived[3].reshape(-1).astype(jnp.float32)
    partner = swapped((gate_proj, up_proj, down_proj), "dp", 0)
    parity = lax.axis_index("dp") % 2
    first = parity == 0
    gate_full = assemble(gate_proj, partner[0], first, 0)
    up_full = assemble(up_proj, partner[1], first, 0)
    down_full = assemble(down_proj, partner[2], first, 1)
    gate_pre = jnp.dot(rows_x, gate_full, preferred_element_type=jnp.float32)
    up_pre = jnp.dot(rows_x, up_full, preferred_element_type=jnp.float32)
    gate_sig = jax.nn.sigmoid(gate_pre)
    activated = gate_pre * gate_sig * up_pre
    hidden = activated.astype(jnp.bfloat16)
    weighted = (route_scale[:, None] * activated).astype(jnp.bfloat16)
    back_hidden = lax.dot_general(
        rows_dy, down_full, (((1,), (1,)), ((), ())), preferred_element_type=jnp.float32
    )
    gate_grad = (keep_rows * jnp.sum(hidden.astype(jnp.float32) * back_hidden, axis=1)).astype(
        jnp.bfloat16
    )
    hidden_grad = route_scale[:, None] * back_hidden
    grad_gate_pre = (hidden_grad * up_pre * gate_sig * (1.0 + gate_pre * (1.0 - gate_sig))).astype(
        jnp.bfloat16
    )
    grad_up_pre = (hidden_grad * gate_pre * gate_sig).astype(jnp.bfloat16)
    transposed = (((1,), (1,)), ((), ()))
    row_grad = (
        lax.dot_general(grad_gate_pre, gate_full, transposed, preferred_element_type=jnp.float32)
        + lax.dot_general(grad_up_pre, up_full, transposed, preferred_element_type=jnp.float32)
    ).astype(jnp.bfloat16)
    leading = (((0,), (0,)), ((), ()))
    grad_gate = lax.dot_general(rows_x, grad_gate_pre, leading, preferred_element_type=jnp.float32)
    grad_up = lax.dot_general(rows_x, grad_up_pre, leading, preferred_element_type=jnp.float32)
    grad_down = lax.dot_general(weighted, rows_dy, leading, preferred_element_type=jnp.float32)
    half_width = width // 2
    own_start = parity * half_width
    other_start = (1 - parity) * half_width
    received = swapped(
        (
            lax.dynamic_slice_in_dim(grad_gate, other_start, half_width, 0),
            lax.dynamic_slice_in_dim(grad_up, other_start, half_width, 0),
            lax.dynamic_slice_in_dim(grad_down, other_start, half_width, 1),
        ),
        "dp",
        0,
    )
    grad_gate_proj = (
        lax.dynamic_slice_in_dim(grad_gate, own_start, half_width, 0) + received[0]
    ).astype(jnp.bfloat16)[None]
    grad_up_proj = (
        lax.dynamic_slice_in_dim(grad_up, own_start, half_width, 0) + received[1]
    ).astype(jnp.bfloat16)[None]
    grad_down_proj = (
        lax.dynamic_slice_in_dim(grad_down, own_start, half_width, 1) + received[2]
    ).astype(jnp.bfloat16)[None]
    going_back = (row_grad.reshape(layout + (width,)), gate_grad.reshape(layout))
    returned = (
        lax.all_to_all(
            lax.all_to_all(going_back[0], "expert", split_axis=0, concat_axis=0, tiled=True),
            "dp",
            split_axis=1,
            concat_axis=1,
            tiled=True,
        ),
        lax.all_to_all(
            lax.all_to_all(going_back[1], "expert", split_axis=0, concat_axis=0, tiled=True),
            "dp",
            split_axis=1,
            concat_axis=1,
            tiled=True,
        ),
    )
    slot_rows = returned[0].reshape(experts_all * capacity, width)
    slot_gates = returned[1].reshape(-1)
    per_assign = slot_rows[destination].reshape(tok_rows, top_count, width)
    grad_tokens = jnp.sum(per_assign.astype(jnp.float32), axis=1).astype(jnp.bfloat16)
    grad_gates = slot_gates[destination].reshape(tok_rows, top_count)
    return (grad_tokens, grad_gates, grad_gate_proj, grad_up_proj, grad_down_proj)


def solution(mesh):
    in_specs = (
        P(("expert", "dp"), None),
        P(("expert", "dp"), None),
        P(("expert", "dp"), None),
        P(("expert", "dp"), None),
        P(("expert", "dp")),
        P(("expert", "dp"), None, None),
        P(("expert", "dp"), None, None),
        P(("expert", "dp"), None, None),
    )
    out_specs = (
        P(("expert", "dp"), None),
        P(("expert", "dp"), None),
        P(("expert", "dp"), None, None),
        P(("expert", "dp"), None, None),
        P(("expert", "dp"), None, None),
    )
    return jax.shard_map(body, mesh=mesh, in_specs=in_specs, out_specs=out_specs, check_vma=False)
```

profile of v0, /device:TPU:2, one launch (start us, length us, event | category | flops | bytes accessed | tf_op | source)
XLA Modules:
  0.0 478.5 jit_solution(9828189084374014296)
XLA Ops:
  7.6 7.6 %gather_fusion.4 = bf16[1280]{0:T(1024)(128)(2,1)S(1)} fusion(bf16[128]{0:T(256)(128)(2,1)S(1)} %convert_element_type.74, s32[2048]{0:T(1024)S(1)} %get-tuple-element.38), kind=kCustom, calls=%fused_computation.4 | custom fusion | bytes 10240 | tf_op jit(solution)/shard_map/gather | solution.py:45
  15.4 8.0 %gather_fusion = bf16[1280]{0:T(1024)(128)(2,1)S(1)} fusion(bf16[1024]{0:T(1024)(128)(2,1)S(1)} %reshape.92, s32[2048]{0:T(1024)S(1)} %get-tuple-element.39), kind=kCustom, calls=%fused_computation | custom fusion | bytes 10240 | tf_op jit(solution)/shard_map/gather | solution.py:44
  24.3 11.5 %all-to-all-start = ((bf16[32,8,5]{2,1,0:T(8,128)(2,1)}), bf16[32,8,5]{2,1,0:T(8,128)(2,1)S(1)}, u32[]{:S(2)}, u32[]{:S(2)}) async-start(bf16[32,8,5]{2,1,0:T(8,128)(2,1)} %reshape.93), calls=%async_computation | async-start | bytes 131072 | tf_op jit(solution)/shard_map/all_to_all | solution.py:69
  36.6 9.2 %all-to-all-done = bf16[32,8,5]{2,1,0:T(8,128)(2,1)S(1)} async-done(((bf16[32,8,5]{2,1,0:T(8,128)(2,1)}), bf16[32,8,5]{2,1,0:T(8,128)(2,1)S(1)}, u32[]{:S(2)}, u32[]{:S(2)}) %all-to-all-start) | async-done | bytes 2592 | tf_op jit(solution)/shard_map/all_to_all | solution.py:69
  50.4 9.3 %all-to-all-done.8 = bf16[32,8,5]{2,1,0:T(8,128)(2,1)S(1)} async-done(((bf16[32,8,5]{2,1,0:T(8,128)(2,1)}), bf16[32,8,5]{2,1,0:T(8,128)(2,1)S(1)}, u32[]{:S(2)}, u32[]{:S(2)}) %all-to-all-start.8) | async-done | bytes 2592 | tf_op jit(solution)/shard_map/all_to_all | solution.py:76
  60.3 4.8 %all-to-all-start.1 = ((bf16[32,8,5]{0,2,1:T(8,128)(2,1)}), bf16[32,8,5]{0,2,1:T(8,128)(2,1)S(1)}, u32[]{:S(2)}, u32[]{:S(2)}) async-start(bf16[32,8,5]{0,2,1:T(8,128)(2,1)} %copy.60), calls=%async_computation.1 | async-start | bytes 32768 | tf_op jit(solution)/shard_map/all_to_all | solution.py:68
  72.3 6.4 %copy.66 = bf16[32,8,5,1024]{3,1,2,0:T(8,128)(2,1)} copy(bf16[32,8,5,1024]{3,2,1,0:T(8,128)(2,1)} %reshape.96) | data formatting | bytes 5242880 | tf_op jit(solution)/shard_map/reshape | solution.py:48
  83.1 5.1 %gather_fusion.1 = bf16[1280,1024]{1,0:T(8,128)(2,1)} fusion(bf16[128,1024]{1,0:T(8,128)(2,1)S(1)} %copy-done.2, s32[2048]{0:T(1024)S(1)} %get-tuple-element.38), kind=kCustom, calls=%fused_computation.1 | custom fusion | bytes 5248000 | tf_op jit(solution)/shard_map/gather | solution.py:49
  88.3 6.0 %reshape.94 = bf16[32,8,5,1024]{3,2,1,0:T(8,128)(2,1)} reshape(bf16[1280,1024]{1,0:T(8,128)(2,1)} %gather_fusion.1) | data formatting | bytes 5242880 | tf_op jit(solution)/shard_map/reshape | solution.py:49
  94.3 6.5 %copy.63 = bf16[32,8,5,1024]{3,1,2,0:T(8,128)(2,1)} copy(bf16[32,8,5,1024]{3,2,1,0:T(8,128)(2,1)} %reshape.94) | data formatting | bytes 5242880 | tf_op jit(solution)/shard_map/reshape | solution.py:49
  100.8 46.5 %all-to-all-done.4 = bf16[32,8,5,1024]{3,1,2,0:T(8,128)(2,1)S(1)} async-done(((bf16[32,8,5,1024]{3,1,2,0:T(8,128)(2,1)}), bf16[32,8,5,1024]{3,1,2,0:T(8,128)(2,1)S(1)}, u32[]{:S(2)}, u32[]{:S(2)}) %all-to-all-start.4) | async-done | bytes 2621472 | tf_op jit(solution)/shard_map/all_to_all | solution.py:55
  147.2 4.8 %all-to-all-start.2 = ((bf16[32,8,5,1024]{3,1,2,0:T(8,128)(2,1)}), bf16[32,8,5,1024]{3,1,2,0:T(8,128)(2,1)}, u32[]{:S(2)}, u32[]{:S(2)}) async-start(bf16[32,8,5,1024]{3,1,2,0:T(8,128)(2,1)} %copy.63), calls=%async_computation.2 | async-start | bytes 5242880 | tf_op jit(solution)/shard_map/all_to_all | solution.py:62
  155.0 60.3 %all-to-all-done.2 = bf16[32,8,5,1024]{3,1,2,0:T(8,128)(2,1)} async-done(((bf16[32,8,5,1024]{3,1,2,0:T(8,128)(2,1)}), bf16[32,8,5,1024]{3,1,2,0:T(8,128)(2,1)}, u32[]{:S(2)}, u32[]{:S(2)}) %all-to-all-start.2) | async-done | bytes 2621472 | tf_op jit(solution)/shard_map/all_to_all | solution.py:62
  215.3 4.8 %all-to-all-start.5 = ((bf16[32,8,5,1024]{3,0,2,1:T(8,128)(2,1)}), bf16[32,8,5,1024]{3,0,2,1:T(8,128)(2,1)S(1)}, u32[]{:S(2)}, u32[]{:S(2)}) async-start(bf16[32,8,5,1024]{3,0,2,1:T(8,128)(2,1)} %copy.67), calls=%async_computation.5 | async-start | bytes 5242880 | tf_op jit(solution)/shard_map/all_to_all | solution.py:54
  224.8 26.7 %all-to-all-done.5 = bf16[32,8,5,1024]{3,0,2,1:T(8,128)(2,1)S(1)} async-done(((bf16[32,8,5,1024]{3,0,2,1:T(8,128)(2,1)}), bf16[32,8,5,1024]{3,0,2,1:T(8,128)(2,1)S(1)}, u32[]{:S(2)}, u32[]{:S(2)}) %all-to-all-start.5) | async-done | bytes 2621472 | tf_op jit(solution)/shard_map/all_to_all | solution.py:54
  252.9 5.0 %all-to-all-start.3 = ((bf16[32,8,5,1024]{3,0,2,1:T(8,128)(2,1)}), bf16[32,8,5,1024]{3,0,2,1:T(8,128)(2,1)S(1)}, u32[]{:S(2)}, u32[]{:S(2)}) async-start(bf16[32,8,5,1024]{3,0,2,1:T(8,128)(2,1)} %copy.64), calls=%async_computation.3 | async-start | bytes 5242880 | tf_op jit(solution)/shard_map/all_to_all | solution.py:61
  270.9 6.2 %reshape.97 = bf16[1280,1024]{1,0:T(8,128)(2,1)} reshape(bf16[32,8,5,1024]{3,2,1,0:T(8,128)(2,1)} %copy.68) | data formatting | bytes 5242880 | tf_op jit(solution)/shard_map/reshape | solution.py:83
  277.1 12.2 %all-to-all-done.3 = bf16[32,8,5,1024]{3,0,2,1:T(8,128)(2,1)S(1)} async-done(((bf16[32,8,5,1024]{3,0,2,1:T(8,128)(2,1)}), bf16[32,8,5,1024]{3,0,2,1:T(8,128)(2,1)S(1)}, u32[]{:S(2)}, u32[]{:S(2)}) %all-to-all-start.3) | async-done | bytes 2621472 | tf_op jit(solution)/shard_map/all_to_all | solution.py:61
  289.3 4.9 %all-to-all-start.9 = ((bf16[32,8,5]{0,2,1:T(8,128)(2,1)}), bf16[32,8,5]{0,2,1:T(8,128)(2,1)S(1)}, u32[]{:S(2)}, u32[]{:S(2)}) async-start(bf16[32,8,5]{0,2,1:T(8,128)(2,1)} %copy.72), calls=%async_computation.9 | async-start | bytes 32768 | tf_op jit(solution)/shard_map/all_to_all | solution.py:75
  297.8 6.4 %reshape.95 = bf16[1280,1024]{1,0:T(8,128)(2,1)} reshape(bf16[32,8,5,1024]{3,2,1,0:T(8,128)(2,1)} %copy.65) | data formatting | bytes 5242880 | tf_op jit(solution)/shard_map/reshape | solution.py:84
  321.5 4.8 %all-to-all-start.10 = ((bf16[32,8,5]{1,2,0:T(8,128)(2,1)}), bf16[32,8,5]{1,2,0:T(8,128)(2,1)S(1)}, u32[]{:S(2)}, u32[]{:S(2)}) async-start(bf16[32,8,5]{1,2,0:T(8,128)(2,1)} %copy.75), calls=%async_computation.10 | async-start | bytes 131072 | tf_op jit(solution)/shard_map/all_to_all | solution.py:150
  326.3 5.4 %add_convert_fusion = bf16[1280,1024]{1,0:T(8,128)(2,1)S(1)} fusion(f32[1280,1024]{1,0:T(8,128)} %fusion.10, bf16[1280,640]{0,1:T(8,128)(2,1)} %get-tuple-element.26, bf16[512,640]{1,0:T(8,128)(2,1)} %get-tuple-element.33, bf16[512,640]{1,0:T(8,128)(2,1)S(1)} %copy-done.15), kind=kOutput, calls=%fused_computation.7 | convolution fusion | flops 1682964480 | bytes 10813440 | tf_op jit(solution)/shard_map/dot_general | solution.py:112
  334.7 6.4 %copy.69 = bf16[32,8,5,1024]{3,1,2,0:T(8,128)(2,1)} copy(bf16[32,8,5,1024]{3,2,1,0:T(8,128)(2,1)} %reshape.98) | data formatting | bytes 5242880 | tf_op jit(solution)/shard_map/reshape | solution.py:140
  341.1 9.9 %all-to-all-start.6 = ((bf16[32,8,5,1024]{3,1,2,0:T(8,128)(2,1)}), bf16[32,8,5,1024]{3,1,2,0:T(8,128)(2,1)S(1)}, u32[]{:S(2)}, u32[]{:S(2)}) async-start(bf16[32,8,5,1024]{3,1,2,0:T(8,128)(2,1)} %copy.69), calls=%async_computation.6 | async-start | bytes 5242880 | tf_op jit(solution)/shard_map/all_to_all | solution.py:143
  351.0 6.1 %fusion.27 = f32[1024,640]{1,0:T(8,128)} fusion(bf16[1280,1024]{1,0:T(8,128)(2,1)} %reshape.97, bf16[1280,640]{0,1:T(8,128)(2,1)} %copy-done.26), kind=kOutput, calls=%fused_computation.76 | convolution fusion | flops 1677721600 | bytes 6881280 | tf_op jit(solution)/shard_map/dot_general | solution.py:117
  361.4 52.7 %all-to-all-done.6 = bf16[32,8,5,1024]{3,1,2,0:T(8,128)(2,1)S(1)} async-done(((bf16[32,8,5,1024]{3,1,2,0:T(8,128)(2,1)}), bf16[32,8,5,1024]{3,1,2,0:T(8,128)(2,1)S(1)}, u32[]{:S(2)}, u32[]{:S(2)}) %all-to-all-start.6) | async-done | bytes 2621472 | tf_op jit(solution)/shard_map/all_to_all | solution.py:143
  414.1 4.8 %all-to-all-start.11 = ((bf16[32,8,5]{0,2,1:T(8,128)(2,1)}), bf16[32,8,5]{0,2,1:T(8,128)(2,1)S(1)}, u32[]{:S(2)}, u32[]{:S(2)}) async-start(bf16[32,8,5]{0,2,1:T(8,128)(2,1)} %copy.76), calls=%async_computation.11 | async-start | bytes 32768 | tf_op jit(solution)/shard_map/all_to_all | solution.py:149
  424.6 4.8 %all-to-all-start.7 = ((bf16[32,8,5,1024]{3,0,2,1:T(8,128)(2,1)}), bf16[32,8,5,1024]{3,0,2,1:T(8,128)(2,1)S(1)}, u32[]{:S(2)}, u32[]{:S(2)}) async-start(bf16[32,8,5,1024]{3,0,2,1:T(8,128)(2,1)} %copy.70), calls=%async_computation.7 | async-start | bytes 5242880 | tf_op jit(solution)/shard_map/all_to_all | solution.py:142
  439.3 6.8 %gather_fusion.5 = bf16[1024]{0:T(1024)(128)(2,1)S(1)} fusion(bf16[1280]{0:T(1024)(128)(2,1)S(1)} %reshape.102, s32[1024]{0:T(1024)S(1)} %broadcast_clamp_fusion), kind=kCustom, calls=%fused_computation.5 | custom fusion | bytes 8192 | tf_op jit(solution)/shard_map/gather | solution.py:161
  454.5 6.2 %all-to-all-done.7 = bf16[32,8,5,1024]{3,0,2,1:T(8,128)(2,1)S(1)} async-done(((bf16[32,8,5,1024]{3,0,2,1:T(8,128)(2,1)}), bf16[32,8,5,1024]{3,0,2,1:T(8,128)(2,1)S(1)}, u32[]{:S(2)}, u32[]{:S(2)}) %all-to-all-start.7) | async-done | bytes 2621472 | tf_op jit(solution)/shard_map/all_to_all | solution.py:142
  464.3 4.9 %reshape.99 = bf16[1280,1024]{1,0:T(8,128)(2,1)S(1)} reshape(bf16[32,8,5,1024]{3,2,1,0:T(8,128)(2,1)} %copy.71) | data formatting | bytes 5242880 | tf_op jit(solution)/shard_map/reshape | solution.py:157
  469.2 5.3 %gather_fusion.3 = bf16[1024,1024]{1,0:T(8,128)(2,1)} fusion(bf16[1280,1024]{1,0:T(8,128)(2,1)S(1)} %reshape.99, s32[1024]{0:T(1024)S(1)} %broadcast_clamp_fusion), kind=kCustom, calls=%fused_computation.3 | custom fusion | bytes 4198400 | tf_op jit(solution)/shard_map/gather | solution.py:159
  (139 shorter events, 106.8 us)
Async XLA Ops:
  0.6 64.5 %copy-start = (bf16[128,1024]{1,0:T(8,128)(2,1)S(1)}, bf16[128,1024]{1,0:T(8,128)(2,1)}, u32[]{:S(2)}) copy-start(bf16[128,1024]{1,0:T(8,128)(2,1)} %param.8) | copy-start | bytes 786436
  0.6 6.9 %copy-start.25 = (s32[128]{0:T(128)S(1)}, s32[128]{0:T(128)}, u32[]{:S(2)}) copy-start(s32[128]{0:T(128)} %param.12) | copy-start | bytes 1540
  2.9 12.3 %copy-start.24 = (bf16[128,8]{0,1:T(8,128)(2,1)S(1)}, bf16[128,8]{0,1:T(8,128)(2,1)}, u32[]{:S(2)}) copy-start(bf16[128,8]{0,1:T(8,128)(2,1)} %param.11) | copy-start | bytes 6148
  24.3 21.5 %all-to-all-start = ((bf16[32,8,5]{2,1,0:T(8,128)(2,1)}), bf16[32,8,5]{2,1,0:T(8,128)(2,1)S(1)}, u32[]{:S(2)}, u32[]{:S(2)}) async-start(bf16[32,8,5]{2,1,0:T(8,128)(2,1)} %reshape.93), calls=%async_computation | async-start | bytes 131072 | tf_op jit(solution)/shard_map/all_to_all | solution.py:69
  45.8 13.9 %all-to-all-start.8 = ((bf16[32,8,5]{2,1,0:T(8,128)(2,1)}), bf16[32,8,5]{2,1,0:T(8,128)(2,1)S(1)}, u32[]{:S(2)}, u32[]{:S(2)}) async-start(bf16[32,8,5]{2,1,0:T(8,128)(2,1)} %reshape.101), calls=%async_computation.8 | async-start | bytes 131072 | tf_op jit(solution)/shard_map/all_to_all | solution.py:76
  60.3 18.5 %all-to-all-start.1 = ((bf16[32,8,5]{0,2,1:T(8,128)(2,1)}), bf16[32,8,5]{0,2,1:T(8,128)(2,1)S(1)}, u32[]{:S(2)}, u32[]{:S(2)}) async-start(bf16[32,8,5]{0,2,1:T(8,128)(2,1)} %copy.60), calls=%async_computation.1 | async-start | bytes 32768 | tf_op jit(solution)/shard_map/all_to_all | solution.py:68
  78.8 68.5 %all-to-all-start.4 = ((bf16[32,8,5,1024]{3,1,2,0:T(8,128)(2,1)}), bf16[32,8,5,1024]{3,1,2,0:T(8,128)(2,1)S(1)}, u32[]{:S(2)}, u32[]{:S(2)}) async-start(bf16[32,8,5,1024]{3,1,2,0:T(8,128)(2,1)} %copy.66), calls=%async_computation.4 | async-start | bytes 5242880 | tf_op jit(solution)/shard_map/all_to_all | solution.py:55
  147.2 68.1 %all-to-all-start.2 = ((bf16[32,8,5,1024]{3,1,2,0:T(8,128)(2,1)}), bf16[32,8,5,1024]{3,1,2,0:T(8,128)(2,1)}, u32[]{:S(2)}, u32[]{:S(2)}) async-start(bf16[32,8,5,1024]{3,1,2,0:T(8,128)(2,1)} %copy.63), calls=%async_computation.2 | async-start | bytes 5242880 | tf_op jit(solution)/shard_map/all_to_all | solution.py:62
  215.3 36.2 %all-to-all-start.5 = ((bf16[32,8,5,1024]{3,0,2,1:T(8,128)(2,1)}), bf16[32,8,5,1024]{3,0,2,1:T(8,128)(2,1)S(1)}, u32[]{:S(2)}, u32[]{:S(2)}) async-start(bf16[32,8,5,1024]{3,0,2,1:T(8,128)(2,1)} %copy.67), calls=%async_computation.5 | async-start | bytes 5242880 | tf_op jit(solution)/shard_map/all_to_all | solution.py:54
  224.8 33.1 %copy-start.12 = (bf16[1,512,640]{2,1,0:T(8,128)(2,1)S(1)}, bf16[1,512,640]{2,1,0:T(8,128)(2,1)}, u32[]{:S(2)}) copy-start(bf16[1,512,640]{2,1,0:T(8,128)(2,1)} %param.13) | copy-start | bytes 1966084
  224.8 33.8 %copy-start.21 = (bf16[32,8,5]{2,1,0:T(8,128)(2,1)S(1)}, bf16[32,8,5]{2,1,0:T(8,128)(2,1)}, u32[]{:S(2)}) copy-start(bf16[32,8,5]{2,1,0:T(8,128)(2,1)} %copy-done.20) | copy-start | bytes 7684
  252.9 36.4 %all-to-all-start.3 = ((bf16[32,8,5,1024]{3,0,2,1:T(8,128)(2,1)}), bf16[32,8,5,1024]{3,0,2,1:T(8,128)(2,1)S(1)}, u32[]{:S(2)}, u32[]{:S(2)}) async-start(bf16[32,8,5,1024]{3,0,2,1:T(8,128)(2,1)} %copy.64), calls=%async_computation.3 | async-start | bytes 5242880 | tf_op jit(solution)/shard_map/all_to_all | solution.py:61
  257.9 2.3 collective-permute-start.2
  258.1 4.5 collective-permute-start.1
  258.4 6.6 %collective-permute-start = (bf16[1,640,512]{2,1,0:T(8,128)(2,1)}, bf16[1,640,512]{2,1,0:T(8,128)(2,1)}, u32[]{:S(2)}, u32[]{:S(2)}) collective-permute-start(bf16[1,640,512]{2,1,0:T(8,128)(2,1)} %param.15), channel_id=1, source_target_pairs={{0,1},{1,0},{2,3},{3,2},{4,5},{5,4},{6,7},{7,6},{8,9},{9,8},{10,11... | collective-permute-start | bytes 1966088 | tf_op jit(solution)/shard_map/ppermute | solution.py:10
  259.7 5.3 %copy-start.14 = (bf16[1,640,512]{2,1,0:T(8,128)(2,1)S(1)}, bf16[1,640,512]{2,1,0:T(8,128)(2,1)}, u32[]{:S(2)}) copy-start(bf16[1,640,512]{2,1,0:T(8,128)(2,1)} %param.15) | copy-start | bytes 1966084
  289.3 31.5 %all-to-all-start.9 = ((bf16[32,8,5]{0,2,1:T(8,128)(2,1)}), bf16[32,8,5]{0,2,1:T(8,128)(2,1)S(1)}, u32[]{:S(2)}, u32[]{:S(2)}) async-start(bf16[32,8,5]{0,2,1:T(8,128)(2,1)} %copy.72), calls=%async_computation.9 | async-start | bytes 32768 | tf_op jit(solution)/shard_map/all_to_all | solution.py:75
  297.8 6.4 %copy-start.5 = (bf16[1280,1024]{1,0:T(8,128)(2,1)S(1)}, bf16[1280,1024]{1,0:T(8,128)(2,1)}, u32[]{:S(2)}) copy-start(bf16[1280,1024]{1,0:T(8,128)(2,1)} %reshape.97) | copy-start | bytes 7864324
  297.8 6.4 %copy-start.15 = (bf16[512,640]{1,0:T(8,128)(2,1)S(1)}, bf16[512,640]{1,0:T(8,128)(2,1)}, u32[]{:S(2)}) copy-start(bf16[512,640]{1,0:T(8,128)(2,1)} %get-tuple-element.32) | copy-start | bytes 1966084
  309.6 6.3 %copy-start.29 = (f32[1280,640]{0,1:T(8,128)}, f32[1280,640]{0,1:T(8,128)S(1)}, u32[]{:S(2)}) copy-start(f32[1280,640]{0,1:T(8,128)S(1)} %fusion.11) | copy-start | bytes 9830404
  321.5 19.6 %all-to-all-start.10 = ((bf16[32,8,5]{1,2,0:T(8,128)(2,1)}), bf16[32,8,5]{1,2,0:T(8,128)(2,1)S(1)}, u32[]{:S(2)}, u32[]{:S(2)}) async-start(bf16[32,8,5]{1,2,0:T(8,128)(2,1)} %copy.75), calls=%async_computation.10 | async-start | bytes 131072 | tf_op jit(solution)/shard_map/all_to_all | solution.py:150
  341.1 73.0 %all-to-all-start.6 = ((bf16[32,8,5,1024]{3,1,2,0:T(8,128)(2,1)}), bf16[32,8,5,1024]{3,1,2,0:T(8,128)(2,1)S(1)}, u32[]{:S(2)}, u32[]{:S(2)}) async-start(bf16[32,8,5,1024]{3,1,2,0:T(8,128)(2,1)} %copy.69), calls=%async_computation.6 | async-start | bytes 5242880 | tf_op jit(solution)/shard_map/all_to_all | solution.py:143
  351.0 6.1 %copy-start.9 = (bf16[1280,1024]{1,0:T(8,128)(2,1)S(1)}, bf16[1280,1024]{1,0:T(8,128)(2,1)}, u32[]{:S(2)}) copy-start(bf16[1280,1024]{1,0:T(8,128)(2,1)} %reshape.95) | copy-start | bytes 7864324
  351.0 6.1 %copy-start.28 = (f32[1280,640]{0,1:T(8,128)S(1)}, f32[1280,640]{0,1:T(8,128)}, u32[]{:S(2)}) copy-start(f32[1280,640]{0,1:T(8,128)} %copy-done.27) | copy-start | bytes 9830404
  351.0 6.1 %copy-start.30 = (f32[1280,640]{0,1:T(8,128)S(1)}, f32[1280,640]{0,1:T(8,128)}, u32[]{:S(2)}) copy-start(f32[1280,640]{0,1:T(8,128)} %copy-done.29) | copy-start | bytes 9830404
  414.1 10.4 %all-to-all-start.11 = ((bf16[32,8,5]{0,2,1:T(8,128)(2,1)}), bf16[32,8,5]{0,2,1:T(8,128)(2,1)S(1)}, u32[]{:S(2)}, u32[]{:S(2)}) async-start(bf16[32,8,5]{0,2,1:T(8,128)(2,1)} %copy.76), calls=%async_computation.11 | async-start | bytes 32768 | tf_op jit(solution)/shard_map/all_to_all | solution.py:149
  421.5 25.4 %collective-permute-start.5 = (f32[640,512]{1,0:T(8,128)}, f32[640,512]{1,0:T(8,128)}, u32[]{:S(2)}, u32[]{:S(2)}) collective-permute-start(f32[640,512]{1,0:T(8,128)} %constant_dynamic-slice_fusion), channel_id=1, source_target_pairs={{0,1},{1,0},{2,3},{3,2},{4,5},{5,4},{6,7},{7,6},{8,9},{9,8},{10,11... | collective-permute-start | bytes 3932168 | tf_op jit(solution)/shard_map/ppermute | solution.py:10
  424.6 36.2 %all-to-all-start.7 = ((bf16[32,8,5,1024]{3,0,2,1:T(8,128)(2,1)}), bf16[32,8,5,1024]{3,0,2,1:T(8,128)(2,1)S(1)}, u32[]{:S(2)}, u32[]{:S(2)}) async-start(bf16[32,8,5,1024]{3,0,2,1:T(8,128)(2,1)} %copy.70), calls=%async_computation.7 | async-start | bytes 5242880 | tf_op jit(solution)/shard_map/all_to_all | solution.py:142
  432.0 17.8 %collective-permute-start.4 = (f32[512,640]{1,0:T(8,128)}, f32[512,640]{1,0:T(8,128)}, u32[]{:S(2)}, u32[]{:S(2)}) collective-permute-start(f32[512,640]{1,0:T(8,128)} %constant_dynamic-slice_fusion.1), channel_id=1, source_target_pairs={{0,1},{1,0},{2,3},{3,2},{4,5},{5,4},{6,7},{7,6},{8,9},{9,8},{10,11... | collective-permute-start | bytes 3932168 | tf_op jit(solution)/shard_map/ppermute | solution.py:10
  438.6 13.6 %collective-permute-start.3 = (f32[512,640]{1,0:T(8,128)}, f32[512,640]{1,0:T(8,128)}, u32[]{:S(2)}, u32[]{:S(2)}) collective-permute-start(f32[512,640]{1,0:T(8,128)} %constant_dynamic-slice_fusion.2), channel_id=1, source_target_pairs={{0,1},{1,0},{2,3},{3,2},{4,5},{5,4},{6,7},{7,6},{8,9},{9,8},{10,11... | collective-permute-start | bytes 3932168 | tf_op jit(solution)/shard_map/ppermute | solution.py:10
  446.9 5.3 %copy-start.11 = (f32[1024,640]{1,0:T(8,128)S(1)}, f32[1024,640]{1,0:T(8,128)}, u32[]{:S(2)}) copy-start(f32[1024,640]{1,0:T(8,128)} %copy-done.10) | copy-start | bytes 7864324
  469.2 9.1 %copy-start.1 = (bf16[128,1024]{1,0:T(8,128)(2,1)S(1)}, bf16[128,1024]{1,0:T(8,128)(2,1)}, u32[]{:S(2)}) copy-start(bf16[128,1024]{1,0:T(8,128)(2,1)} %param.8) | copy-start | bytes 786436
  (17 other events, 50.5 us)
where the time goes:
time: 488 us; the launch traced here: 478 us
  waiting for transfers between devices  224 us (46%)
  local copies, waits for them, and re-layouts  131 us (27%)
  starting transfers between devices  69.7 us (14%)
  matrix products  33.8 us (7%)
  other arithmetic  19.2 us (4%)
    all_to_all x1, waiting for transfers between devices, body(): lax.all_to_all(packed[1], 'expert', split_axis=0, concat_axis=0, tiled=True)  60.3 us
    all_to_all x1, waiting for transfers between devices, body(): lax.all_to_all(going_back[0], 'expert', split_axis=0, concat_axis=0, tile...  52.7 us
    all_to_all x1, waiting for transfers between devices, body(): lax.all_to_all(packed[0], 'expert', split_axis=0, concat_axis=0, tiled=True)  46.5 us
    all_to_all x1, waiting for transfers between devices, body(): lax.all_to_all(lax.all_to_all(packed[0], 'expert', split_axis=0, concat_a...  26.7 us
    reshape x2, local copies, waits for them, and re-layouts, body(): out_grad[source_row].reshape(layout + (width,))  12.5 us
    all_to_all x1, waiting for transfers between devices, body(): lax.all_to_all(lax.all_to_all(packed[1], 'expert', split_axis=0, concat_a...  12.2 us
    all_to_all x1, starting transfers between devices, body(): lax.all_to_all(packed[2], 'expert', split_axis=0, concat_axis=0, tiled=True)  11.5 us
    all_to_all x1, starting transfers between devices, body(): lax.all_to_all(going_back[0], 'expert', split_axis=0, concat_axis=0, tile...  9.9 us
  transfers between devices with their start and end apart: 18, of which 9 were waited for; matrix products, arithmetic and copies ran while one was open for 29% of the time, Pallas kernels for 0%

commit v1 on v0

v1 whole, which is shorter than its diff:
```python
import functools

import jax
import jax.numpy as jnp
from jax import lax
from jax.experimental import pallas as pl
from jax.experimental.pallas import tpu as pltpu
from jax.sharding import PartitionSpec as P

MESH = pl.DeviceIdType.MESH
BF = jnp.bfloat16
F32 = jnp.float32

TOK = 128
NZ = 8
NX = 4
CAP = 10
MSG = NZ * CAP
PLANE = NX * NX
SLOTS = PLANE * MSG
GRP = NX * MSG
NN = (((1,), (0,)), ((), ()))
NT = (((1,), (1,)), ((), ()))
TN = (((0,), (0,)), ((), ()))


def mm(a, b, dims):
    return lax.dot_general(a, b, dims, preferred_element_type=F32)


def kernel(
    x_hbm, dy_hbm, gm_hbm, ids_ref, wg_hbm, wu_hbm, wd_hbm,
    gtok_ref, ggate_ref, ogg_hbm, ogu_hbm, ogd_hbm,
    ag, agg, pt, gt, oh, ohg, send, recv, wgu, wd, gu, q, hid, dgu,
    ds0, ds1, ret0, ret1, rs0, rr0, rs1, rr1, wsg, wsd, wrg, wrd, wog, wod, gown,
    in_sem, gm_sem, w_sem, wout_sem,
    ags, agr, agg_s, agg_r, ps, pr, bs, br, rss, rsr, ws, wr, vs, vr,
):
    e = lax.axis_index("expert")
    d = lax.axis_index("dp")
    y, z = e // NZ, e % NZ
    x, core = d // 2, d % 2
    other = 1 - core

    def dev(dx, dy, dz):
        return (((y + dy + NX) % NX) * NZ + (z + dz + NZ) % NZ, ((x + dx + NX) % NX) * 2 + core)

    mate = (e, x * 2 + other)
    half = ag.shape[2]
    chunks = ag.shape[0]
    hcol = half // 2
    hidn = hid.shape[1]

    gcp = pltpu.make_async_copy(gm_hbm, agg.at[0:TOK], gm_sem)
    gcp.start()
    incp = []
    for c in range(chunks):
        src = x_hbm if c < 2 else dy_hbm
        cp = pltpu.make_async_copy(src.at[:, pl.ds((c % 2) * half, half)], ag.at[c, 0:TOK], in_sem.at[c])
        cp.start()
        incp.append(cp)
    wl = [
        pltpu.make_async_copy(wg_hbm.at[0], wgu.at[core, :, 0:hidn], w_sem.at[0]),
        pltpu.make_async_copy(wu_hbm.at[0], wgu.at[core, :, hidn:2 * hidn], w_sem.at[1]),
        pltpu.make_async_copy(wd_hbm.at[0], wd.at[core], w_sem.at[2]),
    ]
    for cp in wl:
        cp.start()

    bar = pltpu.get_barrier_semaphore()
    for dz in (1, -1):
        pl.semaphore_signal(bar, inc=1, device_id=dev(0, 0, dz), device_id_type=MESH)
    pl.semaphore_signal(bar, inc=1, device_id=mate, device_id_type=MESH)
    for j in range(1, PLANE):
        pl.semaphore_signal(bar, inc=1, device_id=dev(j % NX, j // NX, 0), device_id_type=MESH)
    pl.semaphore_wait(bar, PLANE - 1 + 3)

    def remote(src, dst, s, r, to):
        return pltpu.make_async_remote_copy(
            src_ref=src, dst_ref=dst, send_sem=s, recv_sem=r, device_id=to, device_id_type=MESH
        )

    def block(k):
        return pl.ds(k * TOK, TOK)

    def gather_copies(c, s):
        if c < 0:
            up = remote(agg.at[block(s - 1)], agg.at[block(s)], agg_s.at[0, s - 1], agg_r.at[0, s - 1], dev(0, 0, 1))
            if s == 4:
                return [up]
            a, b = (9 - s) % NZ, 8 - s
            return [up, remote(agg.at[block(a)], agg.at[block(b)], agg_s.at[1, s - 1], agg_r.at[1, s - 1], dev(0, 0, -1))]
        a, b = (9 - s) % NZ, 8 - s
        lo = pl.ds(0, hcol) if s == 4 else pl.ds(0, half)
        hi = pl.ds(hcol, hcol) if s == 4 else pl.ds(0, half)
        return [
            remote(ag.at[c, block(s - 1), lo], ag.at[c, block(s), lo], ags.at[c, 0, s - 1], agr.at[c, 0, s - 1], dev(0, 0, 1)),
            remote(ag.at[c, block(a), hi], ag.at[c, block(b), hi], ags.at[c, 1, s - 1], agr.at[c, 1, s - 1], dev(0, 0, -1)),
        ]

    def ag_start(c, s):
        for cp in gather_copies(c, s):
            cp.start()

    def ag_step(c, s):
        for cp in gather_copies(c, s):
            cp.wait_recv()
        if s < 4:
            ag_start(c, s + 1)

    gcp.wait()
    ag_start(-1, 1)
    incp[0].wait()
    ag_start(0, 1)
    wswap = [
        remote(wg_hbm.at[0], wgu.at[core, :, 0:hidn], ws.at[0], wr.at[0], mate),
        remote(wu_hbm.at[0], wgu.at[core, :, hidn:2 * hidn], ws.at[1], wr.at[1], mate),
        remote(wd_hbm.at[0], wd.at[core], ws.at[2], wr.at[2], mate),
    ]
    wrecv = [
        remote(wg_hbm.at[0], wgu.at[other, :, 0:hidn], ws.at[0], wr.at[0], mate),
        remote(wu_hbm.at[0], wgu.at[other, :, hidn:2 * hidn], ws.at[1], wr.at[1], mate),
        remote(wd_hbm.at[0], wd.at[other], ws.at[2], wr.at[2], mate),
    ]
    for cp in wswap:
        cp.start()

    for s in range(1, 4):
        ag_step(-1, s)
        ag_step(0, s)
    incp[1].wait()
    ag_start(1, 1)
    ag_step(-1, 4)

    gall = agg[...]
    gown[...] = gall[0:TOK]
    routed = jnp.where(gall != 0, 1.0, 0.0).astype(BF)
    row = lax.broadcasted_iota(jnp.int32, (TOK, TOK), 0)
    col = lax.broadcasted_iota(jnp.int32, (TOK, TOK), 1)
    wanted = ((y + row // NX) % NX) * (NZ * NX) + z * NX + (x + row % NX) % NX
    pick = jnp.where((row < PLANE) & (col == wanted), 1.0, 0.0).astype(BF)
    earlier = jnp.where(row < col, 1.0, 0.0).astype(BF)
    rt = mm(pick, routed, NT)
    gt[...] = mm(pick, gall, NT)
    for r in range(NZ):
        mine = rt[:, r * TOK:(r + 1) * TOK]
        place = mm(mine.astype(BF), earlier, NN)
        pt[:, r * TOK:(r + 1) * TOK] = jnp.where(mine > 0.5, place, -1.0)

    prow = lax.broadcasted_iota(jnp.int32, (MSG, NZ * TOK), 0)
    pcol = lax.broadcasted_iota(jnp.int32, (MSG, NZ * TOK), 1)
    pattern = jnp.where(prow // CAP == pcol // TOK, prow % CAP, -2).astype(F32)

    def build(j, carry):
        rows = pl.ds(pl.multiple_of(j * MSG, MSG), MSG)
        hit = pattern == pt[pl.ds(j, 1), :]
        oh[rows, :] = jnp.where(hit, 1.0, 0.0).astype(BF)
        ohg[rows, :] = jnp.where(hit, gt[pl.ds(j, 1), :], 0.0).astype(BF)
        return carry

    lax.fori_loop(0, PLANE, build, 0)
    ag_step(0, 4)

    def rows_of(g):
        return pl.ds(pl.multiple_of(g * GRP, GRP), GRP)

    def exchange(src, dst, s, r, g, sign):
        for dx in range(NX):
            rows = pl.ds(pl.multiple_of(g * GRP + dx * MSG, MSG), MSG)
            cp = remote(src.at[rows], dst.at[rows], s.at[g], r.at[g], dev(sign * dx, sign * g, 0))
            if dx == 0:
                @pl.when(g > 0)
                def _():
                    cp.start()

                @pl.when(g == 0)
                def _():
                    pltpu.make_async_copy(src.at[rows], dst.at[rows], r.at[g]).start()
            else:
                cp.start()

    def arrive(dst, r, g):
        pltpu.make_async_copy(dst.at[rows_of(g)], dst.at[rows_of(g)], r.at[g]).wait()

    def sent(src, s):
        for g in range(NX):
            rows = pl.ds(MSG, GRP - MSG) if g == 0 else rows_of(g)
            pltpu.make_async_copy(src.at[rows], src.at[rows], s.at[g]).wait()

    for c in range(chunks):
        sel = oh if c < 2 else ohg
        for g in range(NX):
            res = mm(sel[g * GRP:(g + 1) * GRP, :], ag[c], NN)
            send[c, g * GRP:(g + 1) * GRP, :] = res.astype(BF)
            exchange(send.at[c], recv.at[c], ps.at[c], pr.at[c], jnp.int32(g), 1)
            if c + 1 < chunks:
                ag_step(c + 1, g + 1)
                if g == 1 and c + 2 < chunks:
                    incp[c + 2].wait()
                    ag_start(c + 2, 1)

    for cp in wl:
        cp.wait()
    for cp in wrecv:
        cp.wait_recv()
    for c in range(2):
        for g in range(NX):
            arrive(recv.at[c], pr.at[c], g)

        def first(g, carry):
            part = mm(recv[c, rows_of(g), :], wgu[c], NN)
            if c == 0:
                gu[rows_of(g), :] = part
            else:
                gu[rows_of(g), :] = gu[rows_of(g), :] + part
            return carry

        lax.fori_loop(0, NX, first, 0)

    SUB = 32

    def activation(i, carry):
        rows = pl.ds(pl.multiple_of(i * SUB, SUB), SUB)
        gpre = gu[rows, 0:hidn]
        upre = gu[rows, hidn:2 * hidn]
        sig = jax.nn.sigmoid(gpre)
        swish = gpre * sig
        hid[rows, :] = (swish * upre).astype(BF)
        gu[rows, 0:hidn] = upre * sig * (1.0 + gpre * (1.0 - sig))
        gu[rows, hidn:2 * hidn] = swish
        return carry

    lax.fori_loop(0, SLOTS // SUB, activation, 0)

    for g in range(NX):
        arrive(recv.at[2], pr.at[2], g)

    def back(g, carry):
        q[rows_of(g), :] = mm(recv[2, rows_of(g), :], wd[0], NT)
        return carry

    lax.fori_loop(0, NX, back, 0)

    expert_lane = y * (NZ * NX) + z * NX + x
    lane = lax.broadcasted_iota(jnp.int32, (SUB, TOK), 1)

    def second(g, carry):
        arrive(recv.at[3], pr.at[3], g)
        q[rows_of(g), :] = q[rows_of(g), :] + mm(recv[3, rows_of(g), :], wd[1], NT)

        def grads(i, inner):
            rows = pl.ds(pl.multiple_of(g * GRP + i * SUB, SUB), SUB)
            dh = q[rows, :]
            dgu[rows, 0:hidn] = (dh * gu[rows, 0:hidn]).astype(BF)
            dgu[rows, hidn:2 * hidn] = (dh * gu[rows, hidn:2 * hidn]).astype(BF)
            dot = jnp.sum(dh * hid[rows, :].astype(F32), axis=1, keepdims=True)
            ds0[rows, half:half + TOK] = jnp.where(lane == expert_lane, dot, 0.0).astype(BF)
            return inner

        lax.fori_loop(0, GRP // SUB, grads, 0)
        ds0[rows_of(g), 0:half] = mm(dgu[rows_of(g), :], wgu[0], NT).astype(BF)
        exchange(ds0, ret0, bs.at[0], br.at[0], g, -1)
        return carry

    lax.fori_loop(0, NX, second, 0)

    def third(g, carry):
        ds1[rows_of(g), :] = mm(dgu[rows_of(g), :], wgu[1], NT).astype(BF)
        exchange(ds1, ret1, bs.at[1], br.at[1], g, -1)
        return carry

    lax.fori_loop(0, NX, third, 0)

    MT = 256

    def other_gu(m, carry):
        cols = pl.ds(pl.multiple_of(m * MT, MT), MT)
        wsg[cols, :] = mm(recv[other, :, cols], dgu[...], TN).astype(BF)
        return carry

    lax.fori_loop(0, half // MT, other_gu, 0)
    gcopy = remote(wsg, wrg, vs.at[0], vr.at[0], mate)
    gcopy.start()
    wsd[...] = mm(hid[...], recv[2 + other], TN).astype(BF)
    dcopy = remote(wsd, wrd, vs.at[1], vr.at[1], mate)
    dcopy.start()
    gcopy.wait_recv()

    def own_gu(m, carry):
        cols = pl.ds(pl.multiple_of(m * MT, MT), MT)
        wog[cols, :] = (mm(recv[core, :, cols], dgu[...], TN) + wrg[cols, :].astype(F32)).astype(BF)
        return carry

    lax.fori_loop(0, half // MT, own_gu, 0)
    dcopy.wait_recv()
    wod[...] = (mm(hid[...], recv[2 + core], TN) + wrd[...].astype(F32)).astype(BF)
    outs = [
        pltpu.make_async_copy(wog.at[:, 0:hidn], ogg_hbm.at[0], wout_sem.at[0]),
        pltpu.make_async_copy(wog.at[:, hidn:2 * hidn], ogu_hbm.at[0], wout_sem.at[1]),
        pltpu.make_async_copy(wod, ogd_hbm.at[0], wout_sem.at[2]),
    ]
    for cp in outs:
        cp.start()

    def home(n, ret, width, cut, sbuf, rbuf, at):
        for g in range(NX):
            arrive(ret, br.at[n], g)

        def combine(m, carry):
            cols = pl.ds(pl.multiple_of(m * MT, MT), MT)
            gu[cols, at:at + width] = mm(oh[:, cols], ret[...], TN)
            return carry

        lax.fori_loop(0, NZ * TOK // MT, combine, 0)

        def part(r):
            return gu[r * TOK:(r + 1) * TOK, at:at + width]

        def hop(k, s):
            lanes = pl.ds(0, width)
            if s == 1:
                lanes = pl.ds(0, cut) if k == 0 else pl.ds(cut, width - cut)
            slot = k * 4 + s - 1
            return remote(sbuf.at[slot, :, lanes], rbuf.at[slot, :, lanes], rss.at[n, slot], rsr.at[n, slot],
                          dev(0, 0, -1 if k == 0 else 1))

        def begin(k, s):
            slot = k * 4 + s - 1
            if s == 1:
                full = part(4)
                if k == 0:
                    sbuf[slot, :, 0:cut] = full[:, 0:cut].astype(BF)
                else:
                    sbuf[slot, :, cut:width] = full[:, cut:width].astype(BF)
            else:
                r = 5 - s if k == 0 else 3 + s
                full = part(r)
                if s == 2:
                    if k == 0:
                        sbuf[slot, :, 0:cut] = (full[:, 0:cut] + rbuf[slot - 1, :, 0:cut].astype(F32)).astype(BF)
                        sbuf[slot, :, cut:width] = full[:, cut:width].astype(BF)
                    else:
                        sbuf[slot, :, 0:cut] = full[:, 0:cut].astype(BF)
                        sbuf[slot, :, cut:width] = (full[:, cut:width] + rbuf[slot - 1, :, cut:width].astype(F32)).astype(BF)
                else:
                    sbuf[slot, :, :] = (full + rbuf[slot - 1].astype(F32)).astype(BF)
            hop(k, s).start()

        for k in range(2):
            begin(k, 1)
        for s in range(2, 5):
            for k in range(2):
                hop(k, s - 1).wait_recv()
                begin(k, s)
        for k in range(2):
            hop(k, 4).wait_recv()
        for s in range(1, 5):
            for k in range(2):
                hop(k, s).wait_send()
        return part(0) + rbuf[3].astype(F32) + rbuf[7].astype(F32)

    tot0 = home(0, ret0, half + TOK, 384, rs0, rr0, 0)
    gtok_ref[:, 0:half] = tot0[:, 0:half].astype(BF)
    gate = gown[...].astype(F32)
    table = tot0[:, half:half + TOK] / jnp.where(gate != 0, gate, 1.0)
    lanes = lax.broadcasted_iota(jnp.int32, (TOK, TOK), 1)
    topn = ids_ref.shape[1]
    out = jnp.zeros((TOK, topn), F32)
    which = lax.broadcasted_iota(jnp.int32, (TOK, topn), 1)
    for j in range(topn):
        value = jnp.sum(jnp.where(lanes == ids_ref[:, j:j + 1], table, 0.0), axis=1, keepdims=True)
        out = jnp.where(which == j, value, out)
    ggate_ref[...] = out.astype(BF)

    tot1 = home(1, ret1, half, 256, rs1, rr1, half + TOK)
    gtok_ref[:, half:2 * half] = tot1.astype(BF)

    for c in range(-1, chunks):
        for s in range(1, 5):
            for cp in gather_copies(c, s):
                cp.wait_send()
    for cp in wswap:
        cp.wait_send()
    for c in range(chunks):
        sent(send.at[c], ps.at[c])
    sent(ds0, bs.at[0])
    sent(ds1, bs.at[1])
    gcopy.wait_send()
    dcopy.wait_send()
    for cp in outs:
        cp.wait()


def body(tokens, out_grad, expert_ids, gate_weights, keep_flags, gate_proj, up_proj, down_proj):
    width = tokens.shape[1]
    half = width // 2
    ff = gate_proj.shape[2]
    experts = TOK
    cols = jnp.arange(experts, dtype=jnp.int32)
    gm = jnp.sum(
        jnp.where(expert_ids[:, :, None] == cols[None, None, :], gate_weights.astype(F32)[:, :, None], 0.0), axis=1
    ).astype(BF)
    dyk = out_grad * keep_flags.astype(BF)[:, None]
    any_spec = pl.BlockSpec(memory_space=pl.ANY)
    vmem = pl.BlockSpec(memory_space=pltpu.VMEM)
    dma = pltpu.SemaphoreType.DMA
    shapes = (
        jax.ShapeDtypeStruct(tokens.shape, BF),
        jax.ShapeDtypeStruct(gate_weights.shape, BF),
        jax.ShapeDtypeStruct(gate_proj.shape, BF),
        jax.ShapeDtypeStruct(up_proj.shape, BF),
        jax.ShapeDtypeStruct(down_proj.shape, BF),
    )
    scratch = [
        pltpu.VMEM((4, NZ * TOK, half), BF),
        pltpu.VMEM((NZ * TOK, experts), BF),
        pltpu.VMEM((TOK, NZ * TOK), F32),
        pltpu.VMEM((TOK, NZ * TOK), F32),
        pltpu.VMEM((SLOTS, NZ * TOK), BF),
        pltpu.VMEM((SLOTS, NZ * TOK), BF),
        pltpu.VMEM((4, SLOTS, half), BF),
        pltpu.VMEM((4, SLOTS, half), BF),
        pltpu.VMEM((2, half, 2 * ff), BF),
        pltpu.VMEM((2, ff, half), BF),
        pltpu.VMEM((SLOTS, 2 * ff), F32),
        pltpu.VMEM((SLOTS, ff), F32),
        pltpu.VMEM((SLOTS, ff), BF),
        pltpu.VMEM((SLOTS, 2 * ff), BF),
        pltpu.VMEM((SLOTS, half + TOK), BF),
        pltpu.VMEM((SLOTS, half), BF),
        pltpu.VMEM((SLOTS, half + TOK), BF),
        pltpu.VMEM((SLOTS, half), BF),
        pltpu.VMEM((8, TOK, half + TOK), BF),
        pltpu.VMEM((8, TOK, half + TOK), BF),
        pltpu.VMEM((8, TOK, half), BF),
        pltpu.VMEM((8, TOK, half), BF),
        pltpu.VMEM((half, 2 * ff), BF),
        pltpu.VMEM((ff, half), BF),
        pltpu.VMEM((half, 2 * ff), BF),
        pltpu.VMEM((ff, half), BF),
        pltpu.VMEM((half, 2 * ff), BF),
        pltpu.VMEM((ff, half), BF),
        pltpu.VMEM((TOK, experts), BF),
        dma((4,)), dma, dma((3,)), dma((3,)),
        dma((4, 2, 4)), dma((4, 2, 4)), dma((2, 4)), dma((2, 4)),
        dma((4, NX)), dma((4, NX)), dma((2, NX)), dma((2, NX)),
        dma((2, 8)), dma((2, 8)), dma((3,)), dma((3,)), dma((2,)), dma((2,)),
    ]
    return pl.pallas_call(
        kernel,
        name="experts",
        out_shape=shapes,
        in_specs=[any_spec, any_spec, any_spec, vmem, any_spec, any_spec, any_spec],
        out_specs=(vmem, vmem, any_spec, any_spec, any_spec),
        scratch_shapes=scratch,
        compiler_params=pltpu.CompilerParams(
            collective_id=0, has_side_effects=True, vmem_limit_bytes=64 * 2**20 - 2**19
        ),
    )(tokens, dyk, gm, expert_ids, gate_proj, up_proj, down_proj)


def solution(mesh):
    both = ("expert", "dp")
    in_specs = (
        P(both, None), P(both, None), P(both, None), P(both, None), P(both),
        P(both, None, None), P(both, None, None), P(both, None, None),
    )
    out_specs = (
        P(both, None), P(both, None), P(both, None, None), P(both, None, None), P(both, None, None),
    )
    return jax.shard_map(body, mesh=mesh, in_specs=in_specs, out_specs=out_specs, check_vma=False)
```

time: 488 us -> 184 us (0.38); the launches traced: 478 us -> 181 us
  waiting for transfers between devices: 224 us -> 0 us
  Pallas kernels: 0 us -> 169 us
  local copies, waits for them, and re-layouts: 131 us -> 8.89 us
  starting transfers between devices: 69.7 us -> 0 us
  matrix products: 33.8 us -> 0 us
  other arithmetic: 19.2 us -> 2.47 us
    all_to_all x12 -> x0, waiting for transfers between devices: 223 us -> none  [the longest x1 60.3 us: body(): lax.all_to_all(packed[1], 'expert', split_axis=0, concat_axis=0, tiled=True)]
    pallas_call x0 -> x1, Pallas kernels: none -> 169 us  [body(): pl.pallas_call(kernel, name='experts', out_shape=shapes, in_specs=[any_sp...]
    all_to_all x12 -> x0, starting transfers between devices: 68.4 us -> none  [the longest x1 11.5 us: body(): lax.all_to_all(packed[2], 'expert', split_axis=0, concat_axis=0, tiled=True)]
    reshape x14 -> x0, local copies, waits for them, and re-layouts: 50.7 us -> none  [the longest x2 12.5 us: body(): out_grad[source_row].reshape(layout + (width,))]
    gather x6 -> x0, local copies, waits for them, and re-layouts: 37.1 us -> none  [the longest x1 7.97 us: body(): send_scale = jnp.where(live_slot, scale_half[source], zero_half)]
    dot_general x9 -> x0, matrix products: 33.8 us -> none  [the longest x1 6.11 us: body(): lax.dot_general(rows_x, grad_up_pre, leading, preferred_element_type=jnp....]
    all_to_all x10 -> x0, local copies, waits for them, and re-layouts: 23.6 us -> none  [the longest x1 4.69 us: body(): lax.all_to_all(packed[1], 'expert', split_axis=0, concat_axis=0, tiled=True)]
    broadcast_in_dim x3 -> x0, other arithmetic: 7.62 us -> none  [the longest x1 2.91 us: body(): (lax.dynamic_slice_in_dim(grad_down, own_start, half_width, 1) + received...]
  transfers between devices with their start and end apart: 18 -> 0, of which waited for: 9 -> 0; matrix products, arithmetic and copies ran while one was open for 29% -> 0% of each run, Pallas kernels for 0% -> 0%
where the time goes in v1:
time: 184 us; the launch traced here: 181 us
  Pallas kernels  169 us (92%)
  local copies, waits for them, and re-layouts  8.89 us (5%)
  other arithmetic  2.47 us (1%)
    pallas_call x1, Pallas kernels, body(): pl.pallas_call(kernel, name='experts', out_shape=shapes, in_specs=[any_sp...  169 us
    unnamed x13, local copies, waits for them, and re-layouts  6.67 us

profile of v1, /device:TPU:2, one launch (start us, length us, event | category | flops | bytes accessed | tf_op | source)
XLA Modules:
  0.0 180.9 jit_solution(985479025748193231)
XLA Ops:
  0.6 0.0 copy-start.3
  0.6 0.7 convert_element_type.9
  1.3 0.8 copy.17.ids_ref
  2.1 0.0 copy-start.2
  2.1 0.8 copy.18
  2.9 1.0 select_reduce_fusion.gm_hbm
  3.9 0.0 copy-done.2
  3.9 0.0 copy-done.3
  3.9 0.8 broadcast_multiply_fusion.dy_hbm
  4.7 168.9 %experts.1 = (bf16[128,1024]{1,0:T(8,128)(2,1)}, bf16[128,8]{1,0:T(8,128)(2,1)}, bf16[1,512,640]{2,1,0:T(8,128)(2,1)}, bf16[1,512,640]{2,1,0:T(8,128)(2,1)}, bf16[1,640,512]{2,1,0:T(8,128)(2,1)}) custom-call(bf16[128,1024]{1,0:T(8,128)(2,1)} %x_hbm.1, bf16[128,1024]{1,0:T(8,128)(2,1)} %broadcast_multiply_fusion.dy_hbm, ...), custom_call_target="tpu_custom_call" | custom-call | tf_op jit(solution)/shard_map/experts/pallas_call | solution.py:449
  173.6 1.4 copy.20
  175.0 1.7 copy.25
  176.7 0.0 copy-start.1
  176.7 2.0 %copy.26 = bf16[1,512,640]{2,1,0:T(8,128)(2,1)} copy(bf16[1,512,640]{2,1,0:T(8,128)(2,1)} %get-tuple-element.22) | data formatting | bytes 1310720
  178.7 0.0 copy-done.1
  178.7 0.0 copy-start
  178.7 0.8 copy.27
  179.6 0.5 copy-done
  180.1 0.8 copy.28
Async XLA Ops:
  0.6 3.3 %copy-start.3 = (bf16[128,1024]{1,0:T(8,128)(2,1)S(1)}, bf16[128,1024]{1,0:T(8,128)(2,1)}, u32[]{:S(2)}) copy-start(bf16[128,1024]{1,0:T(8,128)(2,1)} %param.9) | copy-start | bytes 786436
  2.1 1.8 copy-start.2
  176.7 2.0 %copy-start.1 = (bf16[1,512,640]{2,1,0:T(8,128)(2,1)S(1)}, bf16[1,512,640]{2,1,0:T(8,128)(2,1)}, u32[]{:S(2)}) copy-start(bf16[1,512,640]{2,1,0:T(8,128)(2,1)} %get-tuple-element.23) | copy-start | bytes 1966084
  178.7 1.3 copy-start

commit v2 on v1

v2 whole, which is shorter than its diff:
```python
import functools

import jax
import jax.numpy as jnp
from jax import lax
from jax.experimental import pallas as pl
from jax.experimental.pallas import tpu as pltpu
from jax.sharding import PartitionSpec as P

MESH = pl.DeviceIdType.MESH
BF = jnp.bfloat16
F32 = jnp.float32

TOK = 128
NZ = 8
NX = 4
CAP = 10
MSG = NZ * CAP
PLANE = NX * NX
SLOTS = PLANE * MSG
GRP = NX * MSG
FAR = (2, 1, 3, 0)
NN = (((1,), (0,)), ((), ()))
NT = (((1,), (1,)), ((), ()))
TN = (((0,), (0,)), ((), ()))


def mm(a, b, dims):
    return lax.dot_general(a, b, dims, preferred_element_type=F32)


def kernel(
    x_hbm, dy_hbm, ids_ref, gates_ref, keep_ref, wg_hbm, wu_hbm, wd_hbm,
    gtok_hbm, ggate_ref, ogg_hbm, ogu_hbm, ogd_hbm,
    ag0, ag1, ag2, ag3, dyraw, meta, pt, gt, oh, ohg, send, inter, recv, wgu, wd, gu, q, hid, dgu,
    ds0, ds1, rint0, rint1, ret0, ret1, rsa, rra, rsb, rrb, rsc, rrc, wsg, wsd, wrg, wrd, wog, wod, gtok,
    in_sem, w_sem, wout_sem,
    ags, agr, ms, mr, xs, xr, ys, yr, bs, br, cs, cr, rss, rsr, ws, wr, vs, vr,
):
    e = lax.axis_index("expert")
    d = lax.axis_index("dp")
    y, z = e // NZ, e % NZ
    x, core = d // 2, d % 2
    other = 1 - core

    def dev(dx, dy, dz):
        return (((y + dy + NX) % NX) * NZ + (z + dz + NZ) % NZ, ((x + dx + NX) % NX) * 2 + core)

    mate = (e, x * 2 + other)
    half = ag1.shape[1]
    hidn = hid.shape[1]
    nexp = TOK
    ags_bufs = [ag0, ag1, ag2, ag3]
    quarter = half // 2
    chunks = [(0, 0, quarter), (0, quarter, quarter), (1, 0, half), (2, 0, half), (3, 0, quarter), (3, quarter, quarter)]
    starts = [0, 0, 1, 3, 5, 6]
    nchunk = len(chunks)

    incp = [
        pltpu.make_async_copy(x_hbm.at[:, 0:half], ag0.at[0:TOK], in_sem.at[0]),
        pltpu.make_async_copy(x_hbm.at[:, half:2 * half], ag1.at[0:TOK], in_sem.at[1]),
        pltpu.make_async_copy(dy_hbm, dyraw, in_sem.at[2]),
    ]
    for cp in incp:
        cp.start()
    wl = [
        pltpu.make_async_copy(wg_hbm.at[0], wgu.at[core, :, 0:hidn], w_sem.at[0]),
        pltpu.make_async_copy(wu_hbm.at[0], wgu.at[core, :, hidn:2 * hidn], w_sem.at[1]),
        pltpu.make_async_copy(wd_hbm.at[0], wd.at[core], w_sem.at[2]),
    ]

    bar = pltpu.get_barrier_semaphore()
    for dz in range(1, NZ):
        pl.semaphore_signal(bar, inc=1, device_id=dev(0, 0, dz), device_id_type=MESH)
    pl.semaphore_signal(bar, inc=1, device_id=mate, device_id_type=MESH)
    for j in range(1, PLANE):
        pl.semaphore_signal(bar, inc=1, device_id=dev(j % NX, j // NX, 0), device_id_type=MESH)

    topn = ids_ref.shape[0]
    meta[0] = jnp.concatenate([ids_ref[...].astype(F32), gates_ref[...].astype(F32)], axis=0).astype(BF)
    pl.semaphore_wait(bar, PLANE - 1 + NZ)

    def remote(src, dst, s, r, to):
        return pltpu.make_async_remote_copy(
            src_ref=src, dst_ref=dst, send_sem=s, recv_sem=r, device_id=to, device_id_type=MESH
        )

    def block(k):
        return pl.ds(k * TOK, TOK)

    def gather_copies(c, s):
        buf, lane0, lanes = chunks[c]
        ag = ags_bufs[buf]
        a, b = (9 - s) % NZ, 8 - s
        lo = hi = pl.ds(lane0, lanes)
        if s == 4:
            if lanes > nexp:
                lo, hi = pl.ds(lane0, lanes // 2), pl.ds(lane0 + lanes // 2, lanes // 2)
        ways = [
            (ag.at[block(s - 1), lo], ag.at[block(s), lo], ags.at[c, 0, s - 1], agr.at[c, 0, s - 1], dev(0, 0, 1)),
            (ag.at[block(a), hi], ag.at[block(b), hi], ags.at[c, 1, s - 1], agr.at[c, 1, s - 1], dev(0, 0, -1)),
        ]
        return [remote(*way) for way in (ways[c:c + 1] if s == 4 and lanes == nexp else ways)]

    def ag_start(c):
        for cp in gather_copies(c, 1):
            cp.start()

    def ag_step(c, s):
        for cp in gather_copies(c, s):
            cp.wait_recv()
        if s < 4:
            for cp in gather_copies(c, s + 1):
                cp.start()

    tell = [remote(meta.at[0], meta.at[k], ms.at[k], mr.at[k], dev(0, 0, k)) for k in range(1, NZ)]
    for cp in tell:
        cp.start()
    incp[0].wait()
    for c in range(nchunk):
        if starts[c] == 0:
            ag_start(c)
    wswap = [
        remote(wg_hbm.at[0], wgu.at[core, :, 0:hidn], ws.at[0], wr.at[0], mate),
        remote(wu_hbm.at[0], wgu.at[core, :, hidn:2 * hidn], ws.at[1], wr.at[1], mate),
        remote(wd_hbm.at[0], wd.at[core], ws.at[2], wr.at[2], mate),
    ]
    wrecv = [
        remote(wg_hbm.at[0], wgu.at[other, :, 0:hidn], ws.at[0], wr.at[0], mate),
        remote(wu_hbm.at[0], wgu.at[other, :, hidn:2 * hidn], ws.at[1], wr.at[1], mate),
        remote(wd_hbm.at[0], wd.at[other], ws.at[2], wr.at[2], mate),
    ]

    row = lax.broadcasted_iota(jnp.int32, (TOK, TOK), 0)
    col = lax.broadcasted_iota(jnp.int32, (TOK, TOK), 1)
    row16 = lax.broadcasted_iota(jnp.int32, (PLANE, TOK), 0)
    wanted = (((y + row16 // NX) % NX) * (NZ * NX) + z * NX + (x + row16 % NX) % NX).astype(F32)
    earlier = jnp.where(row < col, 1.0, 0.0).astype(BF)

    def route(r):
        told = meta[r].astype(F32)
        mine = jnp.zeros((PLANE, TOK), F32)
        weight = mine
        for j in range(topn):
            hit = wanted == told[j:j + 1, :]
            mine = jnp.where(hit, 1.0, mine)
            weight = jnp.where(hit, told[topn + j:topn + j + 1, :], weight)
        gt[:, r * TOK:(r + 1) * TOK] = weight
        place = mm(mine.astype(BF), earlier, NN)
        pt[:, r * TOK:(r + 1) * TOK] = jnp.where(mine > 0.5, place, -1.0)

    def mask_rows():
        incp[2].wait()
        keep = jnp.where(row == col, keep_ref[...].astype(F32), 0.0).astype(BF)
        ag2[0:TOK, :] = mm(keep, dyraw[:, 0:half], NN).astype(BF)
        ag3[0:TOK, :] = mm(keep, dyraw[:, half:2 * half], NN).astype(BF)

    prow = lax.broadcasted_iota(jnp.int32, (MSG, NZ * TOK), 0)
    pcol = lax.broadcasted_iota(jnp.int32, (MSG, NZ * TOK), 1)
    pattern = jnp.where(prow // CAP == pcol // TOK, prow % CAP, -2).astype(F32)

    def build(j, carry):
        rows = pl.ds(pl.multiple_of(j * MSG, MSG), MSG)
        oh[rows, :] = jnp.where(pattern == pt[pl.ds(j, 1), :], 1.0, 0.0).astype(BF)
        return carry

    def build_gated(j, carry):
        rows = pl.ds(pl.multiple_of(j * MSG, MSG), MSG)
        ohg[rows, :] = jnp.where(pattern == pt[pl.ds(j, 1), :], gt[pl.ds(j, 1), :], 0.0).astype(BF)
        return carry

    def rows_of(g):
        return pl.ds(pl.multiple_of(g * GRP, GRP), GRP)

    def lanes_of(c):
        return pl.ds(chunks[c][1], chunks[c][2])

    def hand_out(c, g):
        buf, at, width = chunks[c]
        sel = oh if buf < 2 else ohg
        res = mm(sel[g * GRP:(g + 1) * GRP, :], ags_bufs[buf][:, at:at + width], NN).astype(BF)
        target, base = (recv, 0) if g == 0 else (inter, (g - 1) * GRP)
        target[buf, base:base + MSG, at:at + width] = res[0:MSG]
        send[buf, g * GRP + MSG:(g + 1) * GRP, at:at + width] = res[MSG:]
        for dx in FAR[:3]:
            remote(send.at[buf, pl.ds(g * GRP + dx * MSG, MSG), lanes_of(c)],
                   target.at[buf, pl.ds(base + dx * MSG, MSG), lanes_of(c)],
                   xs.at[c, g], xr.at[c, g], dev(dx, 0, 0)).start()

    def along_y(c, g):
        buf = chunks[c][0]
        return remote(inter.at[buf, pl.ds((g - 1) * GRP, GRP), lanes_of(c)], recv.at[buf, pl.ds(g * GRP, GRP), lanes_of(c)],
                      ys.at[c, g], yr.at[c, g], dev(0, g, 0))

    def pass_on(c, g):
        came = inter.at[chunks[c][0], pl.ds((g - 1) * GRP + MSG, GRP - MSG), lanes_of(c)]
        pltpu.make_async_copy(came, came, xr.at[c, g]).wait()
        along_y(c, g).start()

    def landed(c, g):
        if g == 0:
            came = recv.at[chunks[c][0], pl.ds(MSG, GRP - MSG), lanes_of(c)]
            pltpu.make_async_copy(came, came, xr.at[c, 0]).wait()
        else:
            along_y(c, g).wait_recv()

    def tick(t, first=0, end=nchunk):
        for c in range(first, end):
            if 1 <= t - starts[c] <= 4:
                ag_step(c, t - starts[c])
        for c in range(first, end):
            if t == starts[c]:
                if c == 3:
                    mask_rows()
                ag_start(c)

    ag_step(0, 1)
    route(0)
    ag_step(1, 1)
    incp[1].wait()
    ag_start(2)
    ag_step(0, 2)
    for cp in tell:
        cp.wait_recv()
    for r in range(1, NZ):
        route(r)
    ag_step(1, 2)
    ag_step(0, 3)
    lax.fori_loop(0, PLANE, build, 0)
    ag_step(2, 1)
    ag_step(1, 3)
    ag_step(0, 4)

    def first_layer(h):
        for c in range(nchunk):
            if chunks[c][0] == h:
                for g in range(NX):
                    landed(c, g)

        def first(g, carry):
            part = mm(recv[h, rows_of(g), :], wgu[h], NN)
            if h == 0:
                gu[rows_of(g), :] = part
            else:
                gu[rows_of(g), :] = gu[rows_of(g), :] + part
            return carry

        lax.fori_loop(0, NX, first, 0)

    SUB = 32

    def activation(i, carry):
        rows = pl.ds(pl.multiple_of(i * SUB, SUB), SUB)
        gpre = gu[rows, 0:hidn]
        upre = gu[rows, hidn:2 * hidn]
        sig = jax.nn.sigmoid(gpre)
        swish = gpre * sig
        hid[rows, :] = (swish * upre).astype(BF)
        gu[rows, 0:hidn] = upre * sig * (1.0 + gpre * (1.0 - sig))
        gu[rows, hidn:2 * hidn] = swish
        return carry

    for c in range(nchunk):
        if c == 1:
            for cp in wl:
                cp.start()
            for cp in wswap:
                cp.start()
        if chunks[c][0] == 2:
            lax.fori_loop(0, PLANE, build_gated, 0)
        ahead = list(range(starts[c] + 5, starts[c + 1] + 5)) if c + 1 < nchunk else []
        for i, g in enumerate(FAR):
            hand_out(c, g)
            if c == 0 and i == 0:
                tick(3, 2)
            if c == 0 and i == 2:
                ag_step(1, 4)
                tick(4, 2)
            if c == nchunk - 2 and i == 0:
                for cp in wl:
                    cp.wait()
                for cp in wrecv:
                    cp.wait_recv()
                first_layer(0)
            if c == nchunk - 1 and i == 0:
                first_layer(1)
            if c == nchunk - 1 and i == 1:
                lax.fori_loop(0, SLOTS // SUB, activation, 0)
            if c > 0 and g > 0:
                pass_on(c - 1, g)
            if i < len(ahead) - 1:
                tick(ahead[i])
        for t in ahead[3:] if len(ahead) > 4 else ahead[-1:]:
            tick(t)

    for g in FAR[:3]:
        pass_on(nchunk - 1, g)

    for g in range(NX):
        landed(3, g)

    def back(g, carry):
        q[rows_of(g), :] = mm(recv[2, rows_of(g), :], wd[0], NT)
        return carry

    lax.fori_loop(0, NX, back, 0)

    expert_lane = y * (NZ * NX) + z * NX + x
    lane = lax.broadcasted_iota(jnp.int32, (SUB, TOK), 1)
    wide = half + nexp
    back_legs = [(ds0, rint0, ret0, 0, wide), (ds1, rint1, ret1, 0, quarter), (ds1, rint1, ret1, quarter, quarter)]

    def send_back(n, g):
        src, mid, end, lane0, lanes = back_legs[n]
        target, base = (end, 0) if g == 0 else (mid, (g - 1) * GRP)
        for dx in FAR[:3]:
            remote(src.at[pl.ds(g * GRP + dx * MSG, MSG), pl.ds(lane0, lanes)],
                   target.at[pl.ds(base + dx * MSG, MSG), pl.ds(lane0, lanes)],
                   bs.at[n, g], br.at[n, g], dev(-dx, 0, 0)).start()

    def back_along_y(n, g):
        _, mid, end, lane0, lanes = back_legs[n]
        return remote(mid.at[pl.ds((g - 1) * GRP, GRP), pl.ds(lane0, lanes)],
                      end.at[pl.ds(g * GRP, GRP), pl.ds(lane0, lanes)], cs.at[n, g], cr.at[n, g], dev(0, -g, 0))

    def pass_back(n, g):
        _, mid, _, lane0, lanes = back_legs[n]
        came = mid.at[pl.ds((g - 1) * GRP + MSG, GRP - MSG), pl.ds(lane0, lanes)]
        pltpu.make_async_copy(came, came, br.at[n, g]).wait()
        back_along_y(n, g).start()

    def returned(n, g):
        _, _, end, lane0, lanes = back_legs[n]
        if g == 0:
            came = end.at[pl.ds(MSG, GRP - MSG), pl.ds(lane0, lanes)]
            pltpu.make_async_copy(came, came, br.at[n, 0]).wait()
        else:
            back_along_y(n, g).wait_recv()

    def keep_or_send(src, mid, end, g, lanes, value):
        target, base = (end, 0) if g == 0 else (mid, (g - 1) * GRP)
        target[base:base + MSG, lanes] = value[0:MSG]
        src[g * GRP + MSG:(g + 1) * GRP, lanes] = value[MSG:]

    def second(g):
        landed(4, g)
        landed(5, g)
        group = slice(g * GRP, (g + 1) * GRP)
        q[group, :] = q[group, :] + mm(recv[3, group, :], wd[1], NT)

        def grads(k, inner):
            rows = pl.ds(pl.multiple_of(g * GRP + k * SUB, SUB), SUB)
            dh = q[rows, :]
            dgu[rows, 0:hidn] = (dh * gu[rows, 0:hidn]).astype(BF)
            dgu[rows, hidn:2 * hidn] = (dh * gu[rows, hidn:2 * hidn]).astype(BF)
            dot = jnp.sum(dh * hid[rows, :].astype(F32), axis=1, keepdims=True)
            ds0[rows, half:wide] = jnp.where(lane == expert_lane, dot, 0.0).astype(BF)
            return inner

        lax.fori_loop(0, GRP // SUB, grads, 0)
        keep_or_send(ds0, rint0, ret0, g, slice(0, half), mm(dgu[group, :], wgu[0], NT).astype(BF))
        target, base = (ret0, 0) if g == 0 else (rint0, (g - 1) * GRP)
        target[base:base + MSG, half:wide] = ds0[g * GRP:g * GRP + MSG, half:wide]
        send_back(0, g)

    def third(g):
        group = slice(g * GRP, (g + 1) * GRP)
        keep_or_send(ds1, rint1, ret1, g, slice(0, half), mm(dgu[group, :], wgu[1], NT).astype(BF))
        send_back(1, g)

    for g in (0, 2, 1, 3):
        second(g)
    for g in FAR:
        third(g)
    for g in FAR:
        send_back(2, g)
    pass_back(0, 2)

    MT = 256

    def other_gu(m, carry):
        cols = pl.ds(pl.multiple_of(m * MT, MT), MT)
        wsg[cols, :] = mm(recv[other, :, cols], dgu[...], TN).astype(BF)
        return carry

    lax.fori_loop(0, half // MT, other_gu, 0)
    gcopy = remote(wsg, wrg, vs.at[0], vr.at[0], mate)
    gcopy.start()
    pass_back(0, 1)
    wsd[...] = mm(hid[...], recv[2 + other], TN).astype(BF)
    dcopy = remote(wsd, wrd, vs.at[1], vr.at[1], mate)
    dcopy.start()

    outs = [
        pltpu.make_async_copy(wog.at[:, 0:hidn], ogg_hbm.at[0], wout_sem.at[0]),
        pltpu.make_async_copy(wog.at[:, hidn:2 * hidn], ogu_hbm.at[0], wout_sem.at[1]),
        pltpu.make_async_copy(wod, ogd_hbm.at[0], wout_sem.at[2]),
    ]

    def own_gu(m, carry):
        cols = pl.ds(pl.multiple_of(m * MT, MT), MT)
        wog[cols, :] = (mm(recv[core, :, cols], dgu[...], TN) + wrg[cols, :].astype(F32)).astype(BF)
        return carry

    def own_grads():
        gcopy.wait_recv()
        lax.fori_loop(0, half // MT, own_gu, 0)
        outs[0].start()
        outs[1].start()
        dcopy.wait_recv()
        wod[...] = (mm(hid[...], recv[2 + core], TN) + wrd[...].astype(F32)).astype(BF)
        outs[2].start()

    legs = [
        (ret0, 0, wide, 3 * nexp, rsa, rra, 0),
        (ret1, 0, quarter, nexp, rsb, rrb, wide),
        (ret1, quarter, quarter, nexp, rsc, rrc, wide + quarter),
    ]

    def part(n, r):
        width, at = legs[n][2], legs[n][6]
        return gu[r * TOK:(r + 1) * TOK, at:at + width]

    def hop(n, k, s):
        _, _, width, cut, sbuf, rbuf, _ = legs[n]
        lanes = pl.ds(0, width)
        if s == 1:
            lanes = pl.ds(0, cut) if k == 0 else pl.ds(cut, width - cut)
        slot = k * 4 + s - 1
        return remote(sbuf.at[slot, :, lanes], rbuf.at[slot, :, lanes], rss.at[n, slot], rsr.at[n, slot],
                      dev(0, 0, -1 if k == 0 else 1))

    def begin(n, k, s):
        _, _, width, cut, sbuf, rbuf, _ = legs[n]
        slot = k * 4 + s - 1
        full = part(n, 4 if s == 1 else (5 - s if k == 0 else 3 + s))
        if s == 1:
            if k == 0:
                sbuf[slot, :, 0:cut] = full[:, 0:cut].astype(BF)
            else:
                sbuf[slot, :, cut:width] = full[:, cut:width].astype(BF)
        elif s == 2 and k == 0:
            sbuf[slot, :, 0:cut] = (full[:, 0:cut] + rbuf[slot - 1, :, 0:cut].astype(F32)).astype(BF)
            sbuf[slot, :, cut:width] = full[:, cut:width].astype(BF)
        elif s == 2:
            sbuf[slot, :, 0:cut] = full[:, 0:cut].astype(BF)
            sbuf[slot, :, cut:width] = (full[:, cut:width] + rbuf[slot - 1, :, cut:width].astype(F32)).astype(BF)
        else:
            sbuf[slot, :, :] = (full + rbuf[slot - 1].astype(F32)).astype(BF)
        hop(n, k, s).start()

    def step(n, s):
        for k in range(2):
            hop(n, k, s - 1).wait_recv()
            begin(n, k, s)

    def leave(n):
        ret, lane0, width, _, _, _, at = legs[n]
        for g in range(NX):
            returned(n, g)

        def combine(i, carry):
            cols = pl.ds(pl.multiple_of(lax.rem(i + 2, 4) * MT, MT), MT)
            gu[cols, at:at + width] = mm(oh[:, cols], ret[:, lane0:lane0 + width], TN)
            return carry

        lax.fori_loop(0, 1, combine, 0)
        for k in range(2):
            begin(n, k, 1)
        lax.fori_loop(1, NZ * TOK // MT, combine, 0)

    def total(n):
        for k in range(2):
            hop(n, k, 4).wait_recv()
        rbuf = legs[n][5]
        return part(n, 0) + rbuf[3].astype(F32) + rbuf[7].astype(F32)

    pass_back(0, 3)

    @pl.when(core == 0)
    def _():
        own_grads()

    for g in FAR[:3]:
        pass_back(1, g)
    for g in FAR[:3]:
        pass_back(2, g)
    leave(0)
    step(0, 2)
    leave(1)
    step(0, 3)
    step(1, 2)
    leave(2)
    step(0, 4)
    step(1, 3)
    step(2, 2)

    @pl.when(core == 1)
    def _():
        own_grads()

    step(2, 3)
    step(1, 4)
    tot0 = total(0)
    gtok[:, 0:half] = tot0[:, 0:half].astype(BF)
    step(2, 4)
    share = jnp.transpose(tot0[:, half:wide])
    for j in range(topn):
        value = jnp.sum(jnp.where(row == ids_ref[j:j + 1, :], share, 0.0), axis=0, keepdims=True)
        ggate_ref[j:j + 1, :] = value / gates_ref[j:j + 1, :].astype(F32)
    tot1 = total(1)
    gtok[:, half:half + quarter] = tot1.astype(BF)
    tot2 = total(2)
    gtok[:, half + quarter:2 * half] = tot2.astype(BF)
    final = pltpu.make_async_copy(gtok, gtok_hbm, in_sem.at[3])
    final.start()

    for c in range(nchunk):
        for s in range(1, 5):
            for cp in gather_copies(c, s):
                cp.wait_send()
    for cp in wswap:
        cp.wait_send()
    for cp in tell:
        cp.wait_send()
    for c in range(nchunk):
        for g in range(NX):
            gone = send.at[chunks[c][0], pl.ds(g * GRP + MSG, GRP - MSG), lanes_of(c)]
            pltpu.make_async_copy(gone, gone, xs.at[c, g]).wait()
            if g > 0:
                along_y(c, g).wait_send()
    for n, (src, _, _, lane0, lanes) in enumerate(back_legs):
        for g in range(NX):
            gone = src.at[pl.ds(g * GRP + MSG, GRP - MSG), pl.ds(lane0, lanes)]
            pltpu.make_async_copy(gone, gone, bs.at[n, g]).wait()
            if g > 0:
                back_along_y(n, g).wait_send()
    gcopy.wait_send()
    dcopy.wait_send()
    for n in range(len(legs)):
        for s in range(1, 5):
            for k in range(2):
                hop(n, k, s).wait_send()
    for cp in outs:
        cp.wait()
    final.wait()


def finish(a0, a1, a2, a3, a4, o0, o1, o2, o3, o4, v0, v2, v3, v4, sem_in, sem_out):
    held = ((a0, v0, o0), (a2, v2, o2), (a3, v3, o3), (a4, v4, o4))
    ins = [pltpu.make_async_copy(a, v, sem_in.at[i]) for i, (a, v, _) in enumerate(held)]
    outs = [pltpu.make_async_copy(v, o, sem_out.at[i]) for i, (_, v, o) in enumerate(held)]
    for cp in ins:
        cp.start()
    o1[...] = a1[...].astype(BF)
    for cp, out in zip(ins, outs):
        cp.wait()
        out.start()
    for out in outs:
        out.wait()


def body(tokens, out_grad, expert_ids, gate_weights, keep_flags, gate_proj, up_proj, down_proj):
    width = tokens.shape[1]
    half = width // 2
    ff = gate_proj.shape[2]
    topn = expert_ids.shape[1]
    nexp = TOK
    wide = half + nexp
    any_spec = pl.BlockSpec(memory_space=pl.ANY)
    vmem = pl.BlockSpec(memory_space=pltpu.VMEM)
    dma = pltpu.SemaphoreType.DMA
    shapes = (
        jax.ShapeDtypeStruct(tokens.shape, BF),
        jax.ShapeDtypeStruct((topn, TOK), F32),
        jax.ShapeDtypeStruct(gate_proj.shape, BF),
        jax.ShapeDtypeStruct(up_proj.shape, BF),
        jax.ShapeDtypeStruct(down_proj.shape, BF),
    )
    scratch = [
        pltpu.VMEM((NZ * TOK, half), BF),
        pltpu.VMEM((NZ * TOK, half), BF),
        pltpu.VMEM((NZ * TOK, half), BF),
        pltpu.VMEM((NZ * TOK, half), BF),
        pltpu.VMEM((TOK, width), BF),
        pltpu.VMEM((NZ, 2 * topn, TOK), BF),
        pltpu.VMEM((PLANE, NZ * TOK), F32),
        pltpu.VMEM((PLANE, NZ * TOK), F32),
        pltpu.VMEM((SLOTS, NZ * TOK), BF),
        pltpu.VMEM((SLOTS, NZ * TOK), BF),
        pltpu.VMEM((4, SLOTS, half), BF),
        pltpu.VMEM((4, SLOTS - GRP, half), BF),
        pltpu.VMEM((4, SLOTS, half), BF),
        pltpu.VMEM((2, half, 2 * ff), BF),
        pltpu.VMEM((2, ff, half), BF),
        pltpu.VMEM((SLOTS, 2 * ff), F32),
        pltpu.VMEM((SLOTS, ff), F32),
        pltpu.VMEM((SLOTS, ff), BF),
        pltpu.VMEM((SLOTS, 2 * ff), BF),
        pltpu.VMEM((SLOTS, wide), BF),
        pltpu.VMEM((SLOTS, half), BF),
        pltpu.VMEM((SLOTS - GRP, wide), BF),
        pltpu.VMEM((SLOTS - GRP, half), BF),
        pltpu.VMEM((SLOTS, wide), BF),
        pltpu.VMEM((SLOTS, half), BF),
        pltpu.VMEM((8, TOK, wide), BF),
        pltpu.VMEM((8, TOK, wide), BF),
        pltpu.VMEM((8, TOK, half // 2), BF),
        pltpu.VMEM((8, TOK, half // 2), BF),
        pltpu.VMEM((8, TOK, half // 2), BF),
        pltpu.VMEM((8, TOK, half // 2), BF),
        pltpu.VMEM((half, 2 * ff), BF),
        pltpu.VMEM((ff, half), BF),
        pltpu.VMEM((half, 2 * ff), BF),
        pltpu.VMEM((ff, half), BF),
        pltpu.VMEM((half, 2 * ff), BF),
        pltpu.VMEM((ff, half), BF),
        pltpu.VMEM((TOK, width), BF),
        dma((4,)), dma((3,)), dma((3,)),
        dma((6, 2, 4)), dma((6, 2, 4)), dma((NZ,)), dma((NZ,)),
        dma((6, NX)), dma((6, NX)), dma((6, NX)), dma((6, NX)), dma((3, NX)), dma((3, NX)), dma((3, NX)), dma((3, NX)),
        dma((3, 8)), dma((3, 8)), dma((3,)), dma((3,)), dma((2,)), dma((2,)),
    ]
    done = pl.pallas_call(
        kernel,
        name="experts",
        out_shape=shapes,
        in_specs=[any_spec, any_spec, vmem, vmem, vmem, any_spec, any_spec, any_spec],
        out_specs=(any_spec, vmem, any_spec, any_spec, any_spec),
        scratch_shapes=scratch,
        compiler_params=pltpu.CompilerParams(
            collective_id=0, has_side_effects=True, vmem_limit_bytes=64 * 2**20 - 2**19
        ),
    )(tokens, out_grad, expert_ids.T, gate_weights.T, keep_flags.reshape(1, TOK), gate_proj, up_proj, down_proj)
    outs = pl.pallas_call(
        finish,
        name="finish",
        out_shape=(shapes[0], jax.ShapeDtypeStruct((topn, TOK), BF)) + shapes[2:],
        in_specs=[any_spec, vmem, any_spec, any_spec, any_spec],
        out_specs=(any_spec, vmem, any_spec, any_spec, any_spec),
        scratch_shapes=[pltpu.VMEM(shapes[i].shape, BF) for i in (0, 2, 3, 4)] + [dma((4,)), dma((4,))],
        compiler_params=pltpu.CompilerParams(vmem_limit_bytes=64 * 2**20 - 2**19),
    )(*done)
    return outs[0], outs[1].T, outs[2], outs[3], outs[4]


def solution(mesh):
    both = ("expert", "dp")
    in_specs = (
        P(both, None), P(both, None), P(both, None), P(both, None), P(both),
        P(both, None, None), P(both, None, None), P(both, None, None),
    )
    out_specs = (
        P(both, None), P(both, None), P(both, None, None), P(both, None, None), P(both, None, None),
    )
    return jax.shard_map(body, mesh=mesh, in_specs=in_specs, out_specs=out_specs, check_vma=False)
```

time: 184 us -> 170 us (0.924); the launches traced: 181 us -> 170 us
  local copies, waits for them, and re-layouts: 8.89 us -> 0 us
  other arithmetic: 2.47 us -> 0 us
    unnamed x13 -> x0, local copies, waits for them, and re-layouts: 6.67 us -> none
    pallas_call x0 -> x1, Pallas kernels: none -> 3.77 us  [body(): pl.pallas_call(finish, name='finish', out_shape=(shapes[0], jax.ShapeDtyp...]
    pallas_call x1, Pallas kernels: 169 us -> 165 us  [body(): pl.pallas_call(kernel, name='experts', out_shape=shapes, in_specs=[any_sp...]
where the time goes in v2:
time: 170 us
  Pallas kernels  169 us (99%)
    pallas_call x1, Pallas kernels, body(): pl.pallas_call(kernel, name='experts', out_shape=shapes, in_specs=[any_sp...  165 us
    pallas_call x1, Pallas kernels, body(): pl.pallas_call(finish, name='finish', out_shape=(shapes[0], jax.ShapeDtyp...  3.77 us

profile of v2, /device:TPU:2, one launch (start us, length us, event | category | flops | bytes accessed | tf_op | source)
XLA Modules:
  0.0 169.9 jit_solution(4574673204367124044)
XLA Ops:
  0.6 165.4 %experts.1 = (bf16[128,1024]{1,0:T(8,128)(2,1)}, f32[8,128]{1,0:T(8,128)}, bf16[1,512,640]{2,1,0:T(8,128)(2,1)}, bf16[1,512,640]{2,1,0:T(8,128)(2,1)}, bf16[1,640,512]{2,1,0:T(8,128)(2,1)}) custom-call(bf16[128,1024]{1,0:T(8,128)(2,1)} %x_hbm.1, bf16[128,1024]{1,0:T(8,128)(2,1)} %dy_hbm.1, s32[8,128]{1,0:T(8,128)} %bitcast.4, bf16[8,128]{1,0:T(8,128)(2,1)} %bitcast.5, ...), custom_call_target="tpu_custom_call" | custom-call | tf_op jit(solution)/shard_map/experts/pallas_call | solution.py:624
  166.0 3.8 %finish.1 = (bf16[128,1024]{1,0:T(8,128)(2,1)}, bf16[8,128]{1,0:T(8,128)(2,1)}, bf16[1,512,640]{2,1,0:T(8,128)(2,1)}, bf16[1,512,640]{2,1,0:T(8,128)(2,1)}, bf16[1,640,512]{2,1,0:T(8,128)(2,1)}) custom-call(bf16[128,1024]{1,0:T(8,128)(2,1)} %get-tuple-element.15.a0, f32[8,128]{1,0:T(8,128)} %get-tuple-element.16.a1, ...), custom_call_target="tpu_custom_call" | custom-call | tf_op jit(solution)/shard_map/finish/pallas_call | solution.py:635

commit v3 on v2

--- a/solution.py
+++ b/solution.py
@@ -32,10 +32,10 @@
 def kernel(
     x_hbm, dy_hbm, ids_ref, gates_ref, keep_ref, wg_hbm, wu_hbm, wd_hbm,
     gtok_hbm, ggate_ref, ogg_hbm, ogu_hbm, ogd_hbm,
-    ag0, ag1, ag2, ag3, dyraw, meta, pt, gt, oh, ohg, send, inter, recv, wgu, wd, gu, q, hid, dgu,
-    ds0, ds1, rint0, rint1, ret0, ret1, rsa, rra, rsb, rrb, rsc, rrc, wsg, wsd, wrg, wrd, wog, wod, gtok,
+    ag0, ag1, ag2, ag3, dyraw, meta, told_out, told_in, pt, gt, oh, ohg, send, inter, recv, wgu, wd, gu, q, hid, dgu,
+    ds0, ds1, rint0, rint1, ret0, ret1, rsa, rra, rsb, rrb, rsc, rrc, rsd, rrd, wsg, wsd, wrg, wrd, wog, wod, gtok,
     in_sem, w_sem, wout_sem,
-    ags, agr, ms, mr, xs, xr, ys, yr, bs, br, cs, cr, rss, rsr, ws, wr, vs, vr,
+    ags, agr, ms, mr, hs, hr, xs, xr, ys, yr, bs, br, cs, cr, rss, rsr, ws, wr, vs, vr,
 ):
     e = lax.axis_index("expert")
     d = lax.axis_index("dp")
@@ -136,6 +136,8 @@
     row16 = lax.broadcasted_iota(jnp.int32, (PLANE, TOK), 0)
     wanted = (((y + row16 // NX) % NX) * (NZ * NX) + z * NX + (x + row16 % NX) % NX).astype(F32)
     earlier = jnp.where(row < col, 1.0, 0.0).astype(BF)
+    col16 = lax.broadcasted_iota(jnp.int32, (PLANE, TOK), 1).astype(F32)
+    pick = jnp.where(col16 == wanted, 1.0, 0.0).astype(BF)
 
     def route(r):
         told = meta[r].astype(F32)
@@ -296,6 +298,21 @@
     for g in FAR[:3]:
         pass_on(nchunk - 1, g)
 
+    for c in range(nchunk):
+        for s in range(1, 5):
+            for cp in gather_copies(c, s):
+                cp.wait_send()
+
+    def turn(m, carry):
+        cols = pl.ds(pl.multiple_of(m * TOK, TOK), TOK)
+        turned = jnp.transpose(oh[:, cols])
+        ag0[cols, :] = turned[:, 0:half]
+        ag1[cols, :] = turned[:, half:2 * half]
+        ag2[cols, 0:SLOTS - 2 * half] = turned[:, 2 * half:SLOTS]
+        return carry
+
+    lax.fori_loop(0, NZ, turn, 0)
+
     for g in range(NX):
         landed(3, g)
 
@@ -308,7 +325,12 @@
     expert_lane = y * (NZ * NX) + z * NX + x
     lane = lax.broadcasted_iota(jnp.int32, (SUB, TOK), 1)
     wide = half + nexp
-    back_legs = [(ds0, rint0, ret0, 0, wide), (ds1, rint1, ret1, 0, quarter), (ds1, rint1, ret1, quarter, quarter)]
+    back_legs = [
+        (ds0, rint0, ret0, 0, nexp + quarter),
+        (ds0, rint0, ret0, nexp + quarter, quarter),
+        (ds1, rint1, ret1, 0, quarter),
+        (ds1, rint1, ret1, quarter, quarter),
+    ]
 
     def send_back(n, g):
         src, mid, end, lane0, lanes = back_legs[n]
@@ -354,27 +376,35 @@
             dgu[rows, 0:hidn] = (dh * gu[rows, 0:hidn]).astype(BF)
             dgu[rows, hidn:2 * hidn] = (dh * gu[rows, hidn:2 * hidn]).astype(BF)
             dot = jnp.sum(dh * hid[rows, :].astype(F32), axis=1, keepdims=True)
-            ds0[rows, half:wide] = jnp.where(lane == expert_lane, dot, 0.0).astype(BF)
+            ds0[rows, 0:nexp] = jnp.where(lane == expert_lane, dot, 0.0).astype(BF)
             return inner
 
         lax.fori_loop(0, GRP // SUB, grads, 0)
-        keep_or_send(ds0, rint0, ret0, g, slice(0, half), mm(dgu[group, :], wgu[0], NT).astype(BF))
+        keep_or_send(ds0, rint0, ret0, g, slice(nexp, wide), mm(dgu[group, :], wgu[0], NT).astype(BF))
         target, base = (ret0, 0) if g == 0 else (rint0, (g - 1) * GRP)
-        target[base:base + MSG, half:wide] = ds0[g * GRP:g * GRP + MSG, half:wide]
-        send_back(0, g)
+        target[base:base + MSG, 0:nexp] = ds0[g * GRP:g * GRP + MSG, 0:nexp]
+        if g > 0:
+            send_back(0, g)
 
     def third(g):
         group = slice(g * GRP, (g + 1) * GRP)
         keep_or_send(ds1, rint1, ret1, g, slice(0, half), mm(dgu[group, :], wgu[1], NT).astype(BF))
-        send_back(1, g)
+        send_back(2, g)
 
     for g in (0, 2, 1, 3):
         second(g)
+    send_back(0, 0)
     for g in FAR:
-        third(g)
+        send_back(1, g)
+    third(2)
+    third(1)
+    pass_back(0, 2)
+    third(3)
+    pass_back(0, 1)
+    third(0)
+    pass_back(0, 3)
     for g in FAR:
-        send_back(2, g)
-    pass_back(0, 2)
+        send_back(3, g)
 
     MT = 256
 
@@ -386,7 +416,8 @@
     lax.fori_loop(0, half // MT, other_gu, 0)
     gcopy = remote(wsg, wrg, vs.at[0], vr.at[0], mate)
     gcopy.start()
-    pass_back(0, 1)
+    pass_back(1, 2)
+    pass_back(1, 1)
     wsd[...] = mm(hid[...], recv[2 + other], TN).astype(BF)
     dcopy = remote(wsd, wrd, vs.at[1], vr.at[1], mate)
     dcopy.start()
@@ -412,9 +443,10 @@
         outs[2].start()
 
     legs = [
-        (ret0, 0, wide, 3 * nexp, rsa, rra, 0),
-        (ret1, 0, quarter, nexp, rsb, rrb, wide),
-        (ret1, quarter, quarter, nexp, rsc, rrc, wide + quarter),
+        (ret0, nexp, quarter, nexp, rsa, rra, 0),
+        (ret0, nexp + quarter, quarter, nexp, rsb, rrb, quarter),
+        (ret1, 0, quarter, nexp, rsc, rrc, half),
+        (ret1, quarter, quarter, nexp, rsd, rrd, half + quarter),
     ]
 
     def part(n, r):
@@ -454,6 +486,28 @@
             hop(n, k, s - 1).wait_recv()
             begin(n, k, s)
 
+    def select(cols, ret, came):
+        return (
+            mm(ag0[cols, :], ret[0:half, came], NN)
+            + mm(ag1[cols, :], ret[half:2 * half, came], NN)
+            + mm(ag2[cols, 0:SLOTS - 2 * half], ret[2 * half:SLOTS, came], NN)
+        )
+
+    def tell_home(r):
+        return remote(told_out.at[r], told_in.at[r], hs.at[r], hr.at[r], dev(0, 0, -r))
+
+    def gates_home():
+        def turn_back(m, carry):
+            cols = pl.ds(pl.multiple_of(m * MT, MT), MT)
+            found = mm(pick, select(cols, ret0, slice(0, nexp)).astype(BF), NT).astype(BF)
+            for r in range(MT // TOK):
+                told_out[m * (MT // TOK) + r] = found[:, r * TOK:(r + 1) * TOK]
+            return carry
+
+        lax.fori_loop(0, NZ * TOK // MT, turn_back, 0)
+        for r in range(1, NZ):
+            tell_home(r).start()
+
     def leave(n):
         ret, lane0, width, _, _, _, at = legs[n]
         for g in range(NX):
@@ -461,7 +515,7 @@
 
         def combine(i, carry):
             cols = pl.ds(pl.multiple_of(lax.rem(i + 2, 4) * MT, MT), MT)
-            gu[cols, at:at + width] = mm(oh[:, cols], ret[:, lane0:lane0 + width], TN)
+            gu[cols, at:at + width] = select(cols, ret, slice(lane0, lane0 + width))
             return carry
 
         lax.fori_loop(0, 1, combine, 0)
@@ -475,18 +529,20 @@
         rbuf = legs[n][5]
         return part(n, 0) + rbuf[3].astype(F32) + rbuf[7].astype(F32)
 
-    pass_back(0, 3)
+    pass_back(1, 3)
+
+    leave(0)
 
     @pl.when(core == 0)
     def _():
         own_grads()
 
     for g in FAR[:3]:
-        pass_back(1, g)
+        pass_back(2, g)
+    step(0, 2)
+    gates_home()
     for g in FAR[:3]:
-        pass_back(2, g)
-    leave(0)
-    step(0, 2)
+        pass_back(3, g)
     leave(1)
     step(0, 3)
     step(1, 2)
@@ -494,35 +550,41 @@
     step(0, 4)
     step(1, 3)
     step(2, 2)
+    leave(3)
+    step(1, 4)
+    step(2, 3)
+    step(3, 2)
+    gtok[:, 0:quarter] = total(0).astype(BF)
+    for r in range(1, NZ):
+        tell_home(r).wait_recv()
+    there = [told_out[0].astype(F32)] + [told_in[r].astype(F32) for r in range(1, NZ)]
+    names = [((y + row16 // NX) % NX) * (NZ * NX) + ((z + r) % NZ) * NX + (x + row16 % NX) % NX for r in range(NZ)]
+    for j in range(topn):
+        value = jnp.zeros((PLANE, TOK), F32)
+        for r in range(NZ):
+            value = jnp.where(names[r] == ids_ref[j:j + 1, :], there[r], value)
+        value = jnp.sum(value, axis=0, keepdims=True)
+        ggate_ref[j:j + 1, :] = value / gates_ref[j:j + 1, :].astype(F32)
 
     @pl.when(core == 1)
     def _():
         own_grads()
 
-    step(2, 3)
-    step(1, 4)
-    tot0 = total(0)
-    gtok[:, 0:half] = tot0[:, 0:half].astype(BF)
     step(2, 4)
-    share = jnp.transpose(tot0[:, half:wide])
-    for j in range(topn):
-        value = jnp.sum(jnp.where(row == ids_ref[j:j + 1, :], share, 0.0), axis=0, keepdims=True)
-        ggate_ref[j:j + 1, :] = value / gates_ref[j:j + 1, :].astype(F32)
-    tot1 = total(1)
-    gtok[:, half:half + quarter] = tot1.astype(BF)
-    tot2 = total(2)
-    gtok[:, half + quarter:2 * half] = tot2.astype(BF)
+    step(3, 3)
+    gtok[:, quarter:half] = total(1).astype(BF)
+    step(3, 4)
+    gtok[:, half:half + quarter] = total(2).astype(BF)
+    gtok[:, half + quarter:2 * half] = total(3).astype(BF)
     final = pltpu.make_async_copy(gtok, gtok_hbm, in_sem.at[3])
     final.start()
 
-    for c in range(nchunk):
-        for s in range(1, 5):
-            for cp in gather_copies(c, s):
-                cp.wait_send()
     for cp in wswap:
         cp.wait_send()
     for cp in tell:
         cp.wait_send()
+    for r in range(1, NZ):
+        tell_home(r).wait_send()
     for c in range(nchunk):
         for g in range(NX):
             gone = send.at[chunks[c][0], pl.ds(g * GRP + MSG, GRP - MSG), lanes_of(c)]
@@ -584,6 +646,8 @@
         pltpu.VMEM((NZ * TOK, half), BF),
         pltpu.VMEM((TOK, width), BF),
         pltpu.VMEM((NZ, 2 * topn, TOK), BF),
+        pltpu.VMEM((NZ, PLANE, TOK), BF),
+        pltpu.VMEM((NZ, PLANE, TOK), BF),
         pltpu.VMEM((PLANE, NZ * TOK), F32),
         pltpu.VMEM((PLANE, NZ * TOK), F32),
         pltpu.VMEM((SLOTS, NZ * TOK), BF),
@@ -603,8 +667,10 @@
         pltpu.VMEM((SLOTS - GRP, half), BF),
         pltpu.VMEM((SLOTS, wide), BF),
         pltpu.VMEM((SLOTS, half), BF),
-        pltpu.VMEM((8, TOK, wide), BF),
-        pltpu.VMEM((8, TOK, wide), BF),
+        pltpu.VMEM((8, TOK, half // 2), BF),
+        pltpu.VMEM((8, TOK, half // 2), BF),
+        pltpu.VMEM((8, TOK, half // 2), BF),
+        pltpu.VMEM((8, TOK, half // 2), BF),
         pltpu.VMEM((8, TOK, half // 2), BF),
         pltpu.VMEM((8, TOK, half // 2), BF),
         pltpu.VMEM((8, TOK, half // 2), BF),
@@ -617,9 +683,9 @@
         pltpu.VMEM((ff, half), BF),
         pltpu.VMEM((TOK, width), BF),
         dma((4,)), dma((3,)), dma((3,)),
-        dma((6, 2, 4)), dma((6, 2, 4)), dma((NZ,)), dma((NZ,)),
-        dma((6, NX)), dma((6, NX)), dma((6, NX)), dma((6, NX)), dma((3, NX)), dma((3, NX)), dma((3, NX)), dma((3, NX)),
-        dma((3, 8)), dma((3, 8)), dma((3,)), dma((3,)), dma((2,)), dma((2,)),
+        dma((6, 2, 4)), dma((6, 2, 4)), dma((NZ,)), dma((NZ,)), dma((NZ,)), dma((NZ,)),
+        dma((6, NX)), dma((6, NX)), dma((6, NX)), dma((6, NX)), dma((4, NX)), dma((4, NX)), dma((4, NX)), dma((4, NX)),
+        dma((4, 8)), dma((4, 8)), dma((3,)), dma((3,)), dma((2,)), dma((2,)),
     ]
     done = pl.pallas_call(
         kernel,

time: 170 us -> 163 us (0.959)
  Pallas kernels: 169 us -> 161 us
    pallas_call x1, Pallas kernels: 165 us -> 158 us  [body(): pl.pallas_call(kernel, name='experts', out_shape=shapes, in_specs=[any_sp...]
where the time goes in v3:
time: 163 us; the launch traced here: 162 us
  Pallas kernels  161 us (99%)
    pallas_call x1, Pallas kernels, body(): pl.pallas_call(kernel, name='experts', out_shape=shapes, in_specs=[any_sp...  158 us
    pallas_call x1, Pallas kernels, body(): pl.pallas_call(finish, name='finish', out_shape=(shapes[0], jax.ShapeDtyp...  3.77 us

profile of v3, /device:TPU:2, one launch (start us, length us, event | category | flops | bytes accessed | tf_op | source)
XLA Modules:
  0.0 162.1 jit_solution(3346194645272256528)
XLA Ops:
  0.6 157.6 %experts.1 = (bf16[128,1024]{1,0:T(8,128)(2,1)}, f32[8,128]{1,0:T(8,128)}, bf16[1,512,640]{2,1,0:T(8,128)(2,1)}, bf16[1,512,640]{2,1,0:T(8,128)(2,1)}, bf16[1,640,512]{2,1,0:T(8,128)(2,1)}) custom-call(bf16[128,1024]{1,0:T(8,128)(2,1)} %x_hbm.1, bf16[128,1024]{1,0:T(8,128)(2,1)} %dy_hbm.1, s32[8,128]{1,0:T(8,128)} %bitcast.4, bf16[8,128]{1,0:T(8,128)(2,1)} %bitcast.5, ...), custom_call_target="tpu_custom_call" | custom-call | tf_op jit(solution)/shard_map/experts/pallas_call | solution.py:690
  158.2 3.8 %finish.1 = (bf16[128,1024]{1,0:T(8,128)(2,1)}, bf16[8,128]{1,0:T(8,128)(2,1)}, bf16[1,512,640]{2,1,0:T(8,128)(2,1)}, bf16[1,512,640]{2,1,0:T(8,128)(2,1)}, bf16[1,640,512]{2,1,0:T(8,128)(2,1)}) custom-call(bf16[128,1024]{1,0:T(8,128)(2,1)} %get-tuple-element.15.a0, f32[8,128]{1,0:T(8,128)} %get-tuple-element.16.a1, ...), custom_call_target="tpu_custom_call" | custom-call | tf_op jit(solution)/shard_map/finish/pallas_call | solution.py:701

commit v4 on v3

--- a/solution.py
+++ b/solution.py
@@ -73,12 +73,13 @@
     for dz in range(1, NZ):
         pl.semaphore_signal(bar, inc=1, device_id=dev(0, 0, dz), device_id_type=MESH)
     pl.semaphore_signal(bar, inc=1, device_id=mate, device_id_type=MESH)
-    for j in range(1, PLANE):
-        pl.semaphore_signal(bar, inc=1, device_id=dev(j % NX, j // NX, 0), device_id_type=MESH)
+    for k in range(1, NX):
+        pl.semaphore_signal(bar, inc=1, device_id=dev(k, 0, 0), device_id_type=MESH)
+        pl.semaphore_signal(bar, inc=1, device_id=dev(0, k, 0), device_id_type=MESH)
 
     topn = ids_ref.shape[0]
     meta[0] = jnp.concatenate([ids_ref[...].astype(F32), gates_ref[...].astype(F32)], axis=0).astype(BF)
-    pl.semaphore_wait(bar, PLANE - 1 + NZ)
+    pl.semaphore_wait(bar, 2 * (NX - 1) + NZ)
 
     def remote(src, dst, s, r, to):
         return pltpu.make_async_remote_copy(

time: 163 us -> 163 us (level)
  no operation moved by 1% of the time
where the time goes in v4:
time: 163 us
  Pallas kernels  162 us (99%)
    pallas_call x1, Pallas kernels, body(): pl.pallas_call(kernel, name='experts', out_shape=shapes, in_specs=[any_sp...  158 us
    pallas_call x1, Pallas kernels, body(): pl.pallas_call(finish, name='finish', out_shape=(shapes[0], jax.ShapeDtyp...  3.77 us

profile of v4, /device:TPU:2, one launch (start us, length us, event | category | flops | bytes accessed | tf_op | source)
XLA Modules:
  0.0 162.8 jit_solution(8445615632096335404)
XLA Ops:
  0.6 158.2 %experts.1 = (bf16[128,1024]{1,0:T(8,128)(2,1)}, f32[8,128]{1,0:T(8,128)}, bf16[1,512,640]{2,1,0:T(8,128)(2,1)}, bf16[1,512,640]{2,1,0:T(8,128)(2,1)}, bf16[1,640,512]{2,1,0:T(8,128)(2,1)}) custom-call(bf16[128,1024]{1,0:T(8,128)(2,1)} %x_hbm.1, bf16[128,1024]{1,0:T(8,128)(2,1)} %dy_hbm.1, s32[8,128]{1,0:T(8,128)} %bitcast.4, bf16[8,128]{1,0:T(8,128)(2,1)} %bitcast.5, ...), custom_call_target="tpu_custom_call" | custom-call | tf_op jit(solution)/shard_map/experts/pallas_call | solution.py:691
  158.8 3.8 %finish.1 = (bf16[128,1024]{1,0:T(8,128)(2,1)}, bf16[8,128]{1,0:T(8,128)(2,1)}, bf16[1,512,640]{2,1,0:T(8,128)(2,1)}, bf16[1,512,640]{2,1,0:T(8,128)(2,1)}, bf16[1,640,512]{2,1,0:T(8,128)(2,1)}) custom-call(bf16[128,1024]{1,0:T(8,128)(2,1)} %get-tuple-element.15.a0, f32[8,128]{1,0:T(8,128)} %get-tuple-element.16.a1, ...), custom_call_target="tpu_custom_call" | custom-call | tf_op jit(solution)/shard_map/finish/pallas_call | solution.py:702

commit v5 on v4

--- a/solution.py
+++ b/solution.py
@@ -610,7 +610,12 @@
 
 
 def finish(a0, a1, a2, a3, a4, o0, o1, o2, o3, o4, v0, v2, v3, v4, sem_in, sem_out):
-    held = ((a0, v0, o0), (a2, v2, o2), (a3, v3, o3), (a4, v4, o4))
+    held = []
+    for a, v, o in ((a2, v2, o2), (a3, v3, o3), (a4, v4, o4), (a0, v0, o0)):
+        if len(a.shape) == 3:
+            a, v, o = a.at[0], v.at[0], o.at[0]
+        rows = a.shape[0] // 2
+        held += [tuple(ref.at[pl.ds(k * rows, rows)] for ref in (a, v, o)) for k in range(2)]
     ins = [pltpu.make_async_copy(a, v, sem_in.at[i]) for i, (a, v, _) in enumerate(held)]
     outs = [pltpu.make_async_copy(v, o, sem_out.at[i]) for i, (_, v, o) in enumerate(held)]
     for cp in ins:
@@ -705,7 +710,7 @@
         out_shape=(shapes[0], jax.ShapeDtypeStruct((topn, TOK), BF)) + shapes[2:],
         in_specs=[any_spec, vmem, any_spec, any_spec, any_spec],
         out_specs=(any_spec, vmem, any_spec, any_spec, any_spec),
-        scratch_shapes=[pltpu.VMEM(shapes[i].shape, BF) for i in (0, 2, 3, 4)] + [dma((4,)), dma((4,))],
+        scratch_shapes=[pltpu.VMEM(shapes[i].shape, BF) for i in (0, 2, 3, 4)] + [dma((8,)), dma((8,))],
         compiler_params=pltpu.CompilerParams(vmem_limit_bytes=64 * 2**20 - 2**19),
     )(*done)
     return outs[0], outs[1].T, outs[2], outs[3], outs[4]

time: 163 us -> 163 us (level)
  no operation moved by 1% of the time
where the time goes in v5:
time: 163 us
  Pallas kernels  162 us (99%)
    pallas_call x1, Pallas kernels, body(): pl.pallas_call(kernel, name='experts', out_shape=shapes, in_specs=[any_sp...  158 us
    pallas_call x1, Pallas kernels, body(): pl.pallas_call(finish, name='finish', out_shape=(shapes[0], jax.ShapeDtyp...  3.72 us

profile of v5, /device:TPU:2, one launch (start us, length us, event | category | flops | bytes accessed | tf_op | source)
XLA Modules:
  0.0 162.7 jit_solution(16300093109663024564)
XLA Ops:
  0.6 158.2 %experts.1 = (bf16[128,1024]{1,0:T(8,128)(2,1)}, f32[8,128]{1,0:T(8,128)}, bf16[1,512,640]{2,1,0:T(8,128)(2,1)}, bf16[1,512,640]{2,1,0:T(8,128)(2,1)}, bf16[1,640,512]{2,1,0:T(8,128)(2,1)}) custom-call(bf16[128,1024]{1,0:T(8,128)(2,1)} %x_hbm.1, bf16[128,1024]{1,0:T(8,128)(2,1)} %dy_hbm.1, s32[8,128]{1,0:T(8,128)} %bitcast.4, bf16[8,128]{1,0:T(8,128)(2,1)} %bitcast.5, ...), custom_call_target="tpu_custom_call" | custom-call | tf_op jit(solution)/shard_map/experts/pallas_call | solution.py:696
  158.8 3.7 %finish.1 = (bf16[128,1024]{1,0:T(8,128)(2,1)}, bf16[8,128]{1,0:T(8,128)(2,1)}, bf16[1,512,640]{2,1,0:T(8,128)(2,1)}, bf16[1,512,640]{2,1,0:T(8,128)(2,1)}, bf16[1,640,512]{2,1,0:T(8,128)(2,1)}) custom-call(bf16[128,1024]{1,0:T(8,128)(2,1)} %get-tuple-element.15.a0, f32[8,128]{1,0:T(8,128)} %get-tuple-element.16.a1, ...), custom_call_target="tpu_custom_call" | custom-call | tf_op jit(solution)/shard_map/finish/pallas_call | solution.py:707
